TPU v7x, 32 devices: a whole 2x2x4 slice. The times are simulated.
32 devices in a mesh: chain: 2 (over y), block: 4 (over x, core), shot: 4 (over z).
Axes of the slice: x: 2, y: 2, z: 4, core: 2. Of those that a mesh axis runs over, the one named last changes fastest.
Arguments:
- courant: float32 [64, 64, 256], P('chain', 'block'), parts along dimension 0, may hold values from 0.04 to 0.18
- snapshots: bfloat16 [32, 4, 32, 64, 256], P(('chain', 'shot'), None, None, 'block'), parts along dimension 0, may hold values from -6 to 6
- residuals: float32 [32, 5, 2048], P(('chain', 'shot')), parts along dimension 0, may hold values from -6 to 6
- receivers: int32 [32, 3, 2048], P(('chain', 'shot')), parts along dimension 0, may hold values from 0 to 255, as said below
- sources: int32 [32, 3], P(('chain', 'shot')), parts along dimension 0, may hold values from 0 to 255, as said below
- snap_steps: int32 [32, 4], P(('chain', 'shot')), parts along dimension 0, may hold values from 0 to 3
- live_counts: int32 [8], P(('chain', 'shot')), parts along dimension 0, may hold values from 1 to 4, as said below
- mass_spectrum: float32 [512, 64], P(('chain', 'block')), parts along dimension 0, may hold values from 0.2 to 5
Outputs:
- scaled_gradient: float32 [64, 64, 256], P(('chain', 'shot'), 'block'), parts along dimension 0
There are 2 independent parts, one for each index of `chain`. A program takes and returns all parts, laid end to end along the dimension named above; each array names one. Nothing has to cross between parts.
Inputs may be any that keep to these rules, and one draw needn't show every extreme that they name: `receivers`: each index lies inside the grid (depth below 32, x below 64, y below 256); every coordinate's largest value is reached. `sources`: each index lies inside the grid (depth below 32, x below 64, y below 256); every coordinate's largest value is reached. `live_counts`: slots from the count on hold no live shot; some group is full.
All inputs are finite; a program needn't handle non-finite values.
Results may differ from a plain program's by a relative error of at most 0.0003.
Values sent between devices are 32-bit elements; how exact they have to be, the bound alone decides.
A program may use at most 64 MiB of HBM per device.

v0:
```python
import math

import jax
import jax.numpy as jnp
from jax import lax
from jax.sharding import PartitionSpec as P

stencil_weights = (-205.0 / 72.0, 8.0 / 5.0, -1.0 / 5.0, 8.0 / 315.0, -1.0 / 560.0)
mute_radius = 6.0


def with_halo(cells, sides, width):
    for axis, dim in sides:
        count = lax.axis_size(axis)
        ends = count - 1
        head = lax.slice_in_dim(cells, 0, width, axis=dim)
        tail = lax.slice_in_dim(cells, cells.shape[dim] - width, cells.shape[dim], axis=dim)
        cells = jnp.concatenate(
            [
                lax.ppermute(tail, axis, [(i, (i + 1) % count) for i in range(ends)]),
                cells,
                lax.ppermute(head, axis, [((i + 1) % count, i) for i in range(ends)]),
            ],
            axis=dim,
        )
    return cells


def laplace_padded(widened):
    lead = [(0, 0)] * (widened.ndim - 3)
    padded = jnp.pad(widened, lead + [(4, 4), (0, 0), (4, 4)])
    depth_cells = widened.shape[-3]
    slab_cells = widened.shape[-2] - 8
    lateral_cells = widened.shape[-1]
    centre = padded[..., 4 : 4 + depth_cells, 4 : 4 + slab_cells, 4 : 4 + lateral_cells]
    accumulated = 3.0 * stencil_weights[0] * centre
    for k in range(1, 5):
        pair = padded[..., 4 + k : 4 + k + depth_cells, 4 : 4 + slab_cells, 4 : 4 + lateral_cells]
        pair = (
            pair
            + padded[..., 4 - k : 4 - k + depth_cells, 4 : 4 + slab_cells, 4 : 4 + lateral_cells]
        )
        pair = (
            pair
            + padded[..., 4 : 4 + depth_cells, 4 + k : 4 + k + slab_cells, 4 : 4 + lateral_cells]
        )
        pair = (
            pair
            + padded[..., 4 : 4 + depth_cells, 4 - k : 4 - k + slab_cells, 4 : 4 + lateral_cells]
        )
        pair = (
            pair
            + padded[..., 4 : 4 + depth_cells, 4 : 4 + slab_cells, 4 + k : 4 + k + lateral_cells]
        )
        pair = (
            pair
            + padded[..., 4 : 4 + depth_cells, 4 : 4 + slab_cells, 4 - k : 4 - k + lateral_cells]
        )
        accumulated = accumulated + stencil_weights[k] * pair
    return accumulated


def fourier_tables(length):
    counting = jnp.arange(length, dtype=jnp.int32)
    phase_index = counting[:, None] * counting[None, :] % length
    angle_table = phase_index.astype(jnp.float32) * (2.0 * math.pi / length)
    return (jnp.cos(angle_table), jnp.sin(angle_table))


def per_device(
    courant, snapshots, residuals, receivers, sources, snap_steps, live_counts, mass_spectrum
):
    depth_cells, slab_cells, lateral_cells = courant.shape
    slot_count = snapshots.shape[0]
    step_count = snap_steps.shape[1]
    block_start = lax.axis_index("block") * slab_cells
    depth_pos = jnp.arange(depth_cells).astype(jnp.float32)[:, None, None]
    across_pos = (block_start + jnp.arange(slab_cells)).astype(jnp.float32)[None, :, None]
    lateral_pos = jnp.arange(lateral_cells).astype(jnp.float32)[None, None, :]
    live_count = live_counts[0]

    def inject_window(receiver_set, values, window_start, window_cells):
        local_x = receiver_set[1] - window_start
        inside = (local_x >= 0) & (local_x < window_cells)
        clipped = jnp.clip(local_x, 0, window_cells - 1)
        empty = jnp.zeros((depth_cells, window_cells, lateral_cells), jnp.float32)
        return empty.at[receiver_set[0], clipped, receiver_set[2]].add(
            jnp.where(inside, values, 0.0)
        )

    def inject_traces(receiver_set, values):
        return inject_window(receiver_set, values, block_start, slab_cells)

    def source_mute(source_pos):
        source_float = source_pos.astype(jnp.float32)
        distance = (
            (depth_pos - source_float[0]) ** 2
            + (across_pos - source_float[1]) ** 2
            + (lateral_pos - source_float[2]) ** 2
        )
        return 1.0 - jnp.exp(-distance / (mute_radius * mute_radius))

    def shot_image(slot_index, gradient):
        receiver_set = lax.dynamic_index_in_dim(receivers, slot_index, 0, keepdims=False)
        trace_set = lax.dynamic_index_in_dim(residuals, slot_index, 0, keepdims=False)
        snapshot_set = lax.dynamic_index_in_dim(snapshots, slot_index, 0, keepdims=False)
        step_table = lax.dynamic_index_in_dim(snap_steps, slot_index, 0, keepdims=False)
        source_pos = lax.dynamic_index_in_dim(sources, slot_index, 0, keepdims=False)
        previous = jnp.zeros((depth_cells, slab_cells, lateral_cells), jnp.float32)
        current = inject_traces(receiver_set, trace_set[0])
        gradient_part = jnp.zeros((depth_cells, slab_cells, lateral_cells), jnp.float32)
        for t in range(1, step_count + 1):
            widened = with_halo(current, (("block", 1),), 4)
            advanced = (
                2.0 * current
                - previous
                + courant * laplace_padded(widened)
                + inject_traces(receiver_set, trace_set[t])
            )
            chosen = lax.dynamic_index_in_dim(snapshot_set, step_table[t - 1], 0, keepdims=False)
            gradient_part = gradient_part + advanced * chosen.astype(jnp.float32)
            previous, current = (current, advanced)
        live_flag = (slot_index < live_count).astype(jnp.float32)
        return gradient + live_flag * (source_mute(source_pos) * gradient_part)

    gradient = lax.fori_loop(
        0, slot_count, shot_image, jnp.zeros((depth_cells, slab_cells, lateral_cells), jnp.float32)
    )
    summed = lax.psum_scatter(gradient, "shot", scatter_dimension=0, tiled=True)
    cos_lateral, sin_lateral = fourier_tables(lateral_cells)
    highest = lax.Precision.HIGHEST
    real_lateral = jnp.einsum("zxy,yk->zkx", summed, cos_lateral, precision=highest)
    imag_lateral = -jnp.einsum("zxy,yk->zkx", summed, sin_lateral, precision=highest)
    pencils = lax.all_to_all(
        jnp.stack([real_lateral, imag_lateral]), "block", split_axis=2, concat_axis=3, tiled=True
    )
    across_cells = pencils.shape[3]
    cos_across, sin_across = fourier_tables(across_cells)
    real_part = pencils[0]
    imag_part = pencils[1]
    real_full = jnp.einsum("zkx,xa->zka", real_part, cos_across, precision=highest) + jnp.einsum(
        "zkx,xa->zka", imag_part, sin_across, precision=highest
    )
    imag_full = jnp.einsum("zkx,xa->zka", imag_part, cos_across, precision=highest) - jnp.einsum(
        "zkx,xa->zka", real_part, sin_across, precision=highest
    )
    real_full = real_full * mass_spectrum[None]
    imag_full = imag_full * mass_spectrum[None]
    real_back = jnp.einsum("zka,ax->zkx", real_full, cos_across, precision=highest) - jnp.einsum(
        "zka,ax->zkx", imag_full, sin_across, precision=highest
    )
    imag_back = jnp.einsum("zka,ax->zkx", imag_full, cos_across, precision=highest) + jnp.einsum(
        "zka,ax->zkx", real_full, sin_across, precision=highest
    )
    returned = lax.all_to_all(
        jnp.stack([real_back, imag_back]), "block", split_axis=3, concat_axis=2, tiled=True
    )
    spatial = jnp.einsum("zkx,ky->zxy", returned[0], cos_lateral, precision=highest) - jnp.einsum(
        "zkx,ky->zxy", returned[1], sin_lateral, precision=highest
    )
    return spatial / float(across_cells * lateral_cells)


def solution(mesh):
    in_specs = (
        P("chain", "block", None),
        P(("chain", "shot"), None, None, "block", None),
        P(("chain", "shot"), None, None),
        P(("chain", "shot"), None, None),
        P(("chain", "shot"), None),
        P(("chain", "shot"), None),
        P(("chain", "shot")),
        P(("chain", "block"), None),
    )
    out_specs = P(("chain", "shot"), "block", None)
    return jax.shard_map(
        per_device, mesh=mesh, in_specs=in_specs, out_specs=out_specs, check_vma=False
    )
```

profile of v0, /device:TPU:25, one launch (start us, length us, event | category | flops | bytes accessed | tf_op | source)
XLA Modules:
  0.0 559.6 jit_solution(5071576707455053343)
XLA Ops:
  6.5 487.3 %while.19 = (s32[]{:T(128)}, f32[32,16,256]{2,1,0:T(8,128)S(1)}, s32[]{:T(128)}, s32[4,3]{1,0:T(4,128)}, s32[4,3,2048]{2,0,1:T(4,128)}, /*index=5*/s32[]{:T(128)...) while((s32[]{:T(128)}, f32[32,16,256]{2,1,0:T(8,128)S(1)}, ...), condition=%wide.region_6.7_spmd.clone.clone.clone, body=%wide.region_0.6_spmd.clone.clone.clone.sunk | while | flops 37076392 | bytes 85679520 | solution.py:126
  10.6 11.4 %scatter_custom_fusion.28 = f32[131072]{0:T(1024)S(1)} fusion(s32[2048]{0:T(1024)S(1)} %broadcast_select_fusion.2, f32[2048]{0:T(1024)S(1)} %bitcast.230, f32[]{:T(128)} %constant.460.clone.14..sunk), kind=kCustom, calls=%fused_computation.193.clone.1 | custom fusion | flops 2048 | bytes 524292 | tf_op jit(solution)/shard_map/while
  22.2 2.6 collective-permute-start.1
  24.8 3.0 collective-permute-start
  34.3 11.7 %scatter_fusion = f32[131072]{0:T(1024)S(1)} fusion(f32[131072]{0:T(1024)S(1)} %bitcast.210, s32[2048]{0:T(1024)S(1)} %broadcast_select_fusion.2, f32[2048]{0:T(1024)S(1)} %bitcast.229), kind=kCustom, calls=%fused_computation.1.clone.clone.clone.clone.1 | custom fusion | flops 2048 | bytes 32768 | tf_op jit(solution)/shard_map/while
  48.9 3.6 collective-permute-start.2
  57.8 11.7 %scatter_fusion.1 = f32[131072]{0:T(1024)S(1)} fusion(f32[131072]{0:T(1024)S(1)} %bitcast.211, s32[2048]{0:T(1024)S(1)} %broadcast_select_fusion.2, f32[2048]{0:T(1024)S(1)} %bitcast.228), kind=kCustom, calls=%fused_computation.2.clone.clone.clone.clone.1 | custom fusion | flops 2048 | bytes 32768 | tf_op jit(solution)/shard_map/while
  72.4 4.3 collective-permute-start.4
  79.3 2.5 fusion.266
  82.0 11.7 %scatter_fusion.2 = f32[131072]{0:T(1024)S(1)} fusion(f32[131072]{0:T(1024)S(1)} %bitcast.209, s32[2048]{0:T(1024)S(1)} %broadcast_select_fusion.2, f32[2048]{0:T(1024)S(1)} %bitcast.227), kind=kCustom, calls=%fused_computation.3.clone.clone.clone.clone.1 | custom fusion | flops 2048 | bytes 32768 | tf_op jit(solution)/shard_map/while
  104.6 4.4 collective-permute-start.6
  114.3 11.7 %scatter_fusion.3 = f32[131072]{0:T(1024)S(1)} fusion(f32[131072]{0:T(1024)S(1)} %bitcast.208, s32[2048]{0:T(1024)S(1)} %broadcast_select_fusion.2, f32[2048]{0:T(1024)S(1)} %bitcast.226), kind=kCustom, calls=%fused_computation.4.clone.clone.clone.clone.1 | custom fusion | flops 2048 | bytes 32768 | tf_op jit(solution)/shard_map/while
  131.9 11.4 %scatter_custom_fusion.28 = f32[131072]{0:T(1024)S(1)} fusion(s32[2048]{0:T(1024)S(1)} %broadcast_select_fusion.2, f32[2048]{0:T(1024)S(1)} %bitcast.230, f32[]{:T(128)} %constant.460.clone.14..sunk), kind=kCustom, calls=%fused_computation.193.clone.1 | custom fusion | flops 2048 | bytes 524292 | tf_op jit(solution)/shard_map/while
  145.5 4.4 collective-permute-start
  156.4 11.7 %scatter_fusion = f32[131072]{0:T(1024)S(1)} fusion(f32[131072]{0:T(1024)S(1)} %bitcast.210, s32[2048]{0:T(1024)S(1)} %broadcast_select_fusion.2, f32[2048]{0:T(1024)S(1)} %bitcast.229), kind=kCustom, calls=%fused_computation.1.clone.clone.clone.clone.1 | custom fusion | flops 2048 | bytes 32768 | tf_op jit(solution)/shard_map/while
  170.9 3.6 collective-permute-start.2
  179.9 11.7 %scatter_fusion.1 = f32[131072]{0:T(1024)S(1)} fusion(f32[131072]{0:T(1024)S(1)} %bitcast.211, s32[2048]{0:T(1024)S(1)} %broadcast_select_fusion.2, f32[2048]{0:T(1024)S(1)} %bitcast.228), kind=kCustom, calls=%fused_computation.2.clone.clone.clone.clone.1 | custom fusion | flops 2048 | bytes 32768 | tf_op jit(solution)/shard_map/while
  194.4 4.3 collective-permute-start.4
  201.3 2.5 fusion.266
  204.1 11.7 %scatter_fusion.2 = f32[131072]{0:T(1024)S(1)} fusion(f32[131072]{0:T(1024)S(1)} %bitcast.209, s32[2048]{0:T(1024)S(1)} %broadcast_select_fusion.2, f32[2048]{0:T(1024)S(1)} %bitcast.227), kind=kCustom, calls=%fused_computation.3.clone.clone.clone.clone.1 | custom fusion | flops 2048 | bytes 32768 | tf_op jit(solution)/shard_map/while
  226.6 4.4 collective-permute-start.6
  233.6 2.5 fusion.268
  236.3 11.7 %scatter_fusion.3 = f32[131072]{0:T(1024)S(1)} fusion(f32[131072]{0:T(1024)S(1)} %bitcast.208, s32[2048]{0:T(1024)S(1)} %broadcast_select_fusion.2, f32[2048]{0:T(1024)S(1)} %bitcast.226), kind=kCustom, calls=%fused_computation.4.clone.clone.clone.clone.1 | custom fusion | flops 2048 | bytes 32768 | tf_op jit(solution)/shard_map/while
  253.9 11.4 %scatter_custom_fusion.28 = f32[131072]{0:T(1024)S(1)} fusion(s32[2048]{0:T(1024)S(1)} %broadcast_select_fusion.2, f32[2048]{0:T(1024)S(1)} %bitcast.230, f32[]{:T(128)} %constant.460.clone.14..sunk), kind=kCustom, calls=%fused_computation.193.clone.1 | custom fusion | flops 2048 | bytes 524292 | tf_op jit(solution)/shard_map/while
  267.4 4.4 collective-permute-start
  278.3 11.7 %scatter_fusion = f32[131072]{0:T(1024)S(1)} fusion(f32[131072]{0:T(1024)S(1)} %bitcast.210, s32[2048]{0:T(1024)S(1)} %broadcast_select_fusion.2, f32[2048]{0:T(1024)S(1)} %bitcast.229), kind=kCustom, calls=%fused_computation.1.clone.clone.clone.clone.1 | custom fusion | flops 2048 | bytes 32768 | tf_op jit(solution)/shard_map/while
  292.9 3.6 collective-permute-start.2
  301.8 11.7 %scatter_fusion.1 = f32[131072]{0:T(1024)S(1)} fusion(f32[131072]{0:T(1024)S(1)} %bitcast.211, s32[2048]{0:T(1024)S(1)} %broadcast_select_fusion.2, f32[2048]{0:T(1024)S(1)} %bitcast.228), kind=kCustom, calls=%fused_computation.2.clone.clone.clone.clone.1 | custom fusion | flops 2048 | bytes 32768 | tf_op jit(solution)/shard_map/while
  316.3 4.3 collective-permute-start.4
  323.2 2.5 fusion.266
  326.0 11.7 %scatter_fusion.2 = f32[131072]{0:T(1024)S(1)} fusion(f32[131072]{0:T(1024)S(1)} %bitcast.209, s32[2048]{0:T(1024)S(1)} %broadcast_select_fusion.2, f32[2048]{0:T(1024)S(1)} %bitcast.227), kind=kCustom, calls=%fused_computation.3.clone.clone.clone.clone.1 | custom fusion | flops 2048 | bytes 32768 | tf_op jit(solution)/shard_map/while
  348.6 4.4 collective-permute-start.6
  355.5 2.5 fusion.268
  358.2 11.7 %scatter_fusion.3 = f32[131072]{0:T(1024)S(1)} fusion(f32[131072]{0:T(1024)S(1)} %bitcast.208, s32[2048]{0:T(1024)S(1)} %broadcast_select_fusion.2, f32[2048]{0:T(1024)S(1)} %bitcast.226), kind=kCustom, calls=%fused_computation.4.clone.clone.clone.clone.1 | custom fusion | flops 2048 | bytes 32768 | tf_op jit(solution)/shard_map/while
  375.8 11.4 %scatter_custom_fusion.28 = f32[131072]{0:T(1024)S(1)} fusion(s32[2048]{0:T(1024)S(1)} %broadcast_select_fusion.2, f32[2048]{0:T(1024)S(1)} %bitcast.230, f32[]{:T(128)} %constant.460.clone.14..sunk), kind=kCustom, calls=%fused_computation.193.clone.1 | custom fusion | flops 2048 | bytes 524292 | tf_op jit(solution)/shard_map/while
  389.3 4.4 collective-permute-start
  400.2 11.7 %scatter_fusion = f32[131072]{0:T(1024)S(1)} fusion(f32[131072]{0:T(1024)S(1)} %bitcast.210, s32[2048]{0:T(1024)S(1)} %broadcast_select_fusion.2, f32[2048]{0:T(1024)S(1)} %bitcast.229), kind=kCustom, calls=%fused_computation.1.clone.clone.clone.clone.1 | custom fusion | flops 2048 | bytes 32768 | tf_op jit(solution)/shard_map/while
  414.8 3.6 collective-permute-start.2
  423.7 11.7 %scatter_fusion.1 = f32[131072]{0:T(1024)S(1)} fusion(f32[131072]{0:T(1024)S(1)} %bitcast.211, s32[2048]{0:T(1024)S(1)} %broadcast_select_fusion.2, f32[2048]{0:T(1024)S(1)} %bitcast.228), kind=kCustom, calls=%fused_computation.2.clone.clone.clone.clone.1 | custom fusion | flops 2048 | bytes 32768 | tf_op jit(solution)/shard_map/while
  438.2 4.3 collective-permute-start.4
  445.1 2.5 fusion.266
  447.9 11.7 %scatter_fusion.2 = f32[131072]{0:T(1024)S(1)} fusion(f32[131072]{0:T(1024)S(1)} %bitcast.209, s32[2048]{0:T(1024)S(1)} %broadcast_select_fusion.2, f32[2048]{0:T(1024)S(1)} %bitcast.227), kind=kCustom, calls=%fused_computation.3.clone.clone.clone.clone.1 | custom fusion | flops 2048 | bytes 32768 | tf_op jit(solution)/shard_map/while
  470.5 4.4 collective-permute-start.6
  477.4 2.5 fusion.268
  480.1 11.7 %scatter_fusion.3 = f32[131072]{0:T(1024)S(1)} fusion(f32[131072]{0:T(1024)S(1)} %bitcast.208, s32[2048]{0:T(1024)S(1)} %broadcast_select_fusion.2, f32[2048]{0:T(1024)S(1)} %bitcast.226), kind=kCustom, calls=%fused_computation.4.clone.clone.clone.clone.1 | custom fusion | flops 2048 | bytes 32768 | tf_op jit(solution)/shard_map/while
  494.6 19.9 %reduce-scatter.2.cloned.1.call-done = f32[8,16,256]{2,1,0:T(8,128)} async-done(((f32[32,16,256]{2,1,0:T(8,128)}), f32[8,16,256]{2,1,0:T(8,128)}) %reduce-scatter.2.cloned.1.call-update) | async-done | bytes 131088 | tf_op jit(solution)/shard_map/reduce_scatter | solution.py:129
  521.0 8.8 %all_to_all.30 = f32[4,1,16384]{2,1,0:T(1,128)S(1)} all-to-all(f32[4,1,16384]{2,1,0:T(1,128)S(1)} %reshape.431), channel_id=1, replica_groups=mesh['chain'=2,'block'=4,'shot'=4] {'block'}, dimensions={0} | all-to-all | bytes 524288 | tf_op jit(solution)/shard_map/all_to_all | solution.py:134
  538.7 8.4 %all_to_all.31 = f32[4,1,16384]{2,1,0:T(1,128)S(1)} all-to-all(f32[4,1,16384]{2,1,0:T(1,128)S(1)} %reshape.433), channel_id=1, replica_groups=mesh['chain'=2,'block'=4,'shot'=4] {'block'}, dimensions={0} | all-to-all | bytes 524288 | tf_op jit(solution)/shard_map/all_to_all | solution.py:155
  (264 shorter events, 156.3 us)
Async XLA Ops:
  6.5 508.0 %reduce-scatter.2.cloned.1.call-start = ((), (), s32[]{:S(2)}) async-start(), calls=%async_computation.3 | async-start | bytes 655360 | tf_op jit(solution)/shard_map/reduce_scatter | solution.py:129
  22.2 8.4 %collective-permute-start.1 = (f32[32,4,256]{2,1,0:T(4,128)S(1)}, f32[32,4,256]{2,1,0:T(4,128)S(1)}, u32[]{:S(2)}, u32[]{:S(2)}) collective-permute-start(f32[32,4,256]{2,1,0:T(4,128)S(1)} %get-tuple-element.619), channel_id=1, source_target_pairs={{4,0},{8,4},{12,8},{5,1},{9,5},{13,9},{6,2},{10,6},{14,10},{7,3},{... | collective-permute-start | bytes 393224 | tf_op jit(solution)/shard_map/while/body/eval_jaxpr/ppermute | solution.py:22
  24.8 5.8 %collective-permute-start = (f32[32,4,256]{2,1,0:T(4,128)S(1)}, f32[32,4,256]{2,1,0:T(4,128)S(1)}, u32[]{:S(2)}, u32[]{:S(2)}) collective-permute-start(f32[32,4,256]{2,1,0:T(4,128)S(1)} %get-tuple-element.618), channel_id=1, source_target_pairs={{0,4},{4,8},{8,12},{1,5},{5,9},{9,13},{2,6},{6,10},{10,14},{3,7},{... | collective-permute-start | bytes 393224 | tf_op jit(solution)/shard_map/while/body/eval_jaxpr/ppermute | solution.py:20
  30.6 1.0 copy-start
  46.3 6.3 %collective-permute-start.3 = (f32[32,4,256]{2,1,0:T(4,128)S(1)}, f32[32,4,256]{2,1,0:T(4,128)S(1)}, u32[]{:S(2)}, u32[]{:S(2)}) collective-permute-start(f32[32,4,256]{2,1,0:T(4,128)S(1)} %get-tuple-element.622), channel_id=1, source_target_pairs={{4,0},{8,4},{12,8},{5,1},{9,5},{13,9},{6,2},{10,6},{14,10},{7,3},{... | collective-permute-start | bytes 393224 | tf_op jit(solution)/shard_map/while/body/eval_jaxpr/ppermute | solution.py:22
  48.9 5.6 collective-permute-start.2
  69.8 7.0 %collective-permute-start.5 = (f32[32,4,256]{2,1,0:T(4,128)S(1)}, f32[32,4,256]{2,1,0:T(4,128)S(1)}, u32[]{:S(2)}, u32[]{:S(2)}) collective-permute-start(f32[32,4,256]{2,1,0:T(4,128)S(1)} %get-tuple-element.625), channel_id=1, source_target_pairs={{4,0},{8,4},{12,8},{5,1},{9,5},{13,9},{6,2},{10,6},{14,10},{7,3},{... | collective-permute-start | bytes 393224 | tf_op jit(solution)/shard_map/while/body/eval_jaxpr/ppermute | solution.py:22
  72.4 6.3 %collective-permute-start.4 = (f32[32,4,256]{2,1,0:T(4,128)S(1)}, f32[32,4,256]{2,1,0:T(4,128)S(1)}, u32[]{:S(2)}, u32[]{:S(2)}) collective-permute-start(f32[32,4,256]{2,1,0:T(4,128)S(1)} %get-tuple-element.624), channel_id=1, source_target_pairs={{0,4},{4,8},{8,12},{1,5},{5,9},{9,13},{2,6},{6,10},{10,14},{3,7},{... | collective-permute-start | bytes 393224 | tf_op jit(solution)/shard_map/while/body/eval_jaxpr/ppermute | solution.py:20
  94.0 15.0 %collective-permute-start.7 = (f32[32,4,256]{2,1,0:T(4,128)S(1)}, f32[32,4,256]{2,1,0:T(4,128)S(1)}, u32[]{:S(2)}, u32[]{:S(2)}) collective-permute-start(f32[32,4,256]{2,1,0:T(4,128)S(1)} %get-tuple-element.628), channel_id=1, source_target_pairs={{4,0},{8,4},{12,8},{5,1},{9,5},{13,9},{6,2},{10,6},{14,10},{7,3},{... | collective-permute-start | bytes 393224 | tf_op jit(solution)/shard_map/while/body/eval_jaxpr/ppermute | solution.py:22
  104.6 6.3 %collective-permute-start.6 = (f32[32,4,256]{2,1,0:T(4,128)S(1)}, f32[32,4,256]{2,1,0:T(4,128)S(1)}, u32[]{:S(2)}, u32[]{:S(2)}) collective-permute-start(f32[32,4,256]{2,1,0:T(4,128)S(1)} %get-tuple-element.627), channel_id=1, source_target_pairs={{0,4},{4,8},{8,12},{1,5},{5,9},{9,13},{2,6},{6,10},{10,14},{3,7},{... | collective-permute-start | bytes 393224 | tf_op jit(solution)/shard_map/while/body/eval_jaxpr/ppermute | solution.py:20
  143.6 9.1 %collective-permute-start.1 = (f32[32,4,256]{2,1,0:T(4,128)S(1)}, f32[32,4,256]{2,1,0:T(4,128)S(1)}, u32[]{:S(2)}, u32[]{:S(2)}) collective-permute-start(f32[32,4,256]{2,1,0:T(4,128)S(1)} %get-tuple-element.619), channel_id=1, source_target_pairs={{4,0},{8,4},{12,8},{5,1},{9,5},{13,9},{6,2},{10,6},{14,10},{7,3},{... | collective-permute-start | bytes 393224 | tf_op jit(solution)/shard_map/while/body/eval_jaxpr/ppermute | solution.py:22
  145.5 7.2 %collective-permute-start = (f32[32,4,256]{2,1,0:T(4,128)S(1)}, f32[32,4,256]{2,1,0:T(4,128)S(1)}, u32[]{:S(2)}, u32[]{:S(2)}) collective-permute-start(f32[32,4,256]{2,1,0:T(4,128)S(1)} %get-tuple-element.618), channel_id=1, source_target_pairs={{0,4},{4,8},{8,12},{1,5},{5,9},{9,13},{2,6},{6,10},{10,14},{3,7},{... | collective-permute-start | bytes 393224 | tf_op jit(solution)/shard_map/while/body/eval_jaxpr/ppermute | solution.py:20
  152.6 1.0 copy-start
  168.3 6.3 %collective-permute-start.3 = (f32[32,4,256]{2,1,0:T(4,128)S(1)}, f32[32,4,256]{2,1,0:T(4,128)S(1)}, u32[]{:S(2)}, u32[]{:S(2)}) collective-permute-start(f32[32,4,256]{2,1,0:T(4,128)S(1)} %get-tuple-element.622), channel_id=1, source_target_pairs={{4,0},{8,4},{12,8},{5,1},{9,5},{13,9},{6,2},{10,6},{14,10},{7,3},{... | collective-permute-start | bytes 393224 | tf_op jit(solution)/shard_map/while/body/eval_jaxpr/ppermute | solution.py:22
  170.9 5.6 collective-permute-start.2
  191.8 7.0 %collective-permute-start.5 = (f32[32,4,256]{2,1,0:T(4,128)S(1)}, f32[32,4,256]{2,1,0:T(4,128)S(1)}, u32[]{:S(2)}, u32[]{:S(2)}) collective-permute-start(f32[32,4,256]{2,1,0:T(4,128)S(1)} %get-tuple-element.625), channel_id=1, source_target_pairs={{4,0},{8,4},{12,8},{5,1},{9,5},{13,9},{6,2},{10,6},{14,10},{7,3},{... | collective-permute-start | bytes 393224 | tf_op jit(solution)/shard_map/while/body/eval_jaxpr/ppermute | solution.py:22
  194.4 6.3 %collective-permute-start.4 = (f32[32,4,256]{2,1,0:T(4,128)S(1)}, f32[32,4,256]{2,1,0:T(4,128)S(1)}, u32[]{:S(2)}, u32[]{:S(2)}) collective-permute-start(f32[32,4,256]{2,1,0:T(4,128)S(1)} %get-tuple-element.624), channel_id=1, source_target_pairs={{0,4},{4,8},{8,12},{1,5},{5,9},{9,13},{2,6},{6,10},{10,14},{3,7},{... | collective-permute-start | bytes 393224 | tf_op jit(solution)/shard_map/while/body/eval_jaxpr/ppermute | solution.py:20
  216.0 15.0 %collective-permute-start.7 = (f32[32,4,256]{2,1,0:T(4,128)S(1)}, f32[32,4,256]{2,1,0:T(4,128)S(1)}, u32[]{:S(2)}, u32[]{:S(2)}) collective-permute-start(f32[32,4,256]{2,1,0:T(4,128)S(1)} %get-tuple-element.628), channel_id=1, source_target_pairs={{4,0},{8,4},{12,8},{5,1},{9,5},{13,9},{6,2},{10,6},{14,10},{7,3},{... | collective-permute-start | bytes 393224 | tf_op jit(solution)/shard_map/while/body/eval_jaxpr/ppermute | solution.py:22
  226.6 6.3 %collective-permute-start.6 = (f32[32,4,256]{2,1,0:T(4,128)S(1)}, f32[32,4,256]{2,1,0:T(4,128)S(1)}, u32[]{:S(2)}, u32[]{:S(2)}) collective-permute-start(f32[32,4,256]{2,1,0:T(4,128)S(1)} %get-tuple-element.627), channel_id=1, source_target_pairs={{0,4},{4,8},{8,12},{1,5},{5,9},{9,13},{2,6},{6,10},{10,14},{3,7},{... | collective-permute-start | bytes 393224 | tf_op jit(solution)/shard_map/while/body/eval_jaxpr/ppermute | solution.py:20
  265.5 9.1 %collective-permute-start.1 = (f32[32,4,256]{2,1,0:T(4,128)S(1)}, f32[32,4,256]{2,1,0:T(4,128)S(1)}, u32[]{:S(2)}, u32[]{:S(2)}) collective-permute-start(f32[32,4,256]{2,1,0:T(4,128)S(1)} %get-tuple-element.619), channel_id=1, source_target_pairs={{4,0},{8,4},{12,8},{5,1},{9,5},{13,9},{6,2},{10,6},{14,10},{7,3},{... | collective-permute-start | bytes 393224 | tf_op jit(solution)/shard_map/while/body/eval_jaxpr/ppermute | solution.py:22
  267.4 7.2 %collective-permute-start = (f32[32,4,256]{2,1,0:T(4,128)S(1)}, f32[32,4,256]{2,1,0:T(4,128)S(1)}, u32[]{:S(2)}, u32[]{:S(2)}) collective-permute-start(f32[32,4,256]{2,1,0:T(4,128)S(1)} %get-tuple-element.618), channel_id=1, source_target_pairs={{0,4},{4,8},{8,12},{1,5},{5,9},{9,13},{2,6},{6,10},{10,14},{3,7},{... | collective-permute-start | bytes 393224 | tf_op jit(solution)/shard_map/while/body/eval_jaxpr/ppermute | solution.py:20
  274.5 1.0 copy-start
  290.2 6.3 %collective-permute-start.3 = (f32[32,4,256]{2,1,0:T(4,128)S(1)}, f32[32,4,256]{2,1,0:T(4,128)S(1)}, u32[]{:S(2)}, u32[]{:S(2)}) collective-permute-start(f32[32,4,256]{2,1,0:T(4,128)S(1)} %get-tuple-element.622), channel_id=1, source_target_pairs={{4,0},{8,4},{12,8},{5,1},{9,5},{13,9},{6,2},{10,6},{14,10},{7,3},{... | collective-permute-start | bytes 393224 | tf_op jit(solution)/shard_map/while/body/eval_jaxpr/ppermute | solution.py:22
  292.9 5.6 collective-permute-start.2
  313.7 7.0 %collective-permute-start.5 = (f32[32,4,256]{2,1,0:T(4,128)S(1)}, f32[32,4,256]{2,1,0:T(4,128)S(1)}, u32[]{:S(2)}, u32[]{:S(2)}) collective-permute-start(f32[32,4,256]{2,1,0:T(4,128)S(1)} %get-tuple-element.625), channel_id=1, source_target_pairs={{4,0},{8,4},{12,8},{5,1},{9,5},{13,9},{6,2},{10,6},{14,10},{7,3},{... | collective-permute-start | bytes 393224 | tf_op jit(solution)/shard_map/while/body/eval_jaxpr/ppermute | solution.py:22
  316.3 6.3 %collective-permute-start.4 = (f32[32,4,256]{2,1,0:T(4,128)S(1)}, f32[32,4,256]{2,1,0:T(4,128)S(1)}, u32[]{:S(2)}, u32[]{:S(2)}) collective-permute-start(f32[32,4,256]{2,1,0:T(4,128)S(1)} %get-tuple-element.624), channel_id=1, source_target_pairs={{0,4},{4,8},{8,12},{1,5},{5,9},{9,13},{2,6},{6,10},{10,14},{3,7},{... | collective-permute-start | bytes 393224 | tf_op jit(solution)/shard_map/while/body/eval_jaxpr/ppermute | solution.py:20
  337.9 15.0 %collective-permute-start.7 = (f32[32,4,256]{2,1,0:T(4,128)S(1)}, f32[32,4,256]{2,1,0:T(4,128)S(1)}, u32[]{:S(2)}, u32[]{:S(2)}) collective-permute-start(f32[32,4,256]{2,1,0:T(4,128)S(1)} %get-tuple-element.628), channel_id=1, source_target_pairs={{4,0},{8,4},{12,8},{5,1},{9,5},{13,9},{6,2},{10,6},{14,10},{7,3},{... | collective-permute-start | bytes 393224 | tf_op jit(solution)/shard_map/while/body/eval_jaxpr/ppermute | solution.py:22
  348.6 6.3 %collective-permute-start.6 = (f32[32,4,256]{2,1,0:T(4,128)S(1)}, f32[32,4,256]{2,1,0:T(4,128)S(1)}, u32[]{:S(2)}, u32[]{:S(2)}) collective-permute-start(f32[32,4,256]{2,1,0:T(4,128)S(1)} %get-tuple-element.627), channel_id=1, source_target_pairs={{0,4},{4,8},{8,12},{1,5},{5,9},{9,13},{2,6},{6,10},{10,14},{3,7},{... | collective-permute-start | bytes 393224 | tf_op jit(solution)/shard_map/while/body/eval_jaxpr/ppermute | solution.py:20
  387.4 9.1 %collective-permute-start.1 = (f32[32,4,256]{2,1,0:T(4,128)S(1)}, f32[32,4,256]{2,1,0:T(4,128)S(1)}, u32[]{:S(2)}, u32[]{:S(2)}) collective-permute-start(f32[32,4,256]{2,1,0:T(4,128)S(1)} %get-tuple-element.619), channel_id=1, source_target_pairs={{4,0},{8,4},{12,8},{5,1},{9,5},{13,9},{6,2},{10,6},{14,10},{7,3},{... | collective-permute-start | bytes 393224 | tf_op jit(solution)/shard_map/while/body/eval_jaxpr/ppermute | solution.py:22
  389.3 7.2 %collective-permute-start = (f32[32,4,256]{2,1,0:T(4,128)S(1)}, f32[32,4,256]{2,1,0:T(4,128)S(1)}, u32[]{:S(2)}, u32[]{:S(2)}) collective-permute-start(f32[32,4,256]{2,1,0:T(4,128)S(1)} %get-tuple-element.618), channel_id=1, source_target_pairs={{0,4},{4,8},{8,12},{1,5},{5,9},{9,13},{2,6},{6,10},{10,14},{3,7},{... | collective-permute-start | bytes 393224 | tf_op jit(solution)/shard_map/while/body/eval_jaxpr/ppermute | solution.py:20
  396.4 1.0 copy-start
  412.1 6.3 %collective-permute-start.3 = (f32[32,4,256]{2,1,0:T(4,128)S(1)}, f32[32,4,256]{2,1,0:T(4,128)S(1)}, u32[]{:S(2)}, u32[]{:S(2)}) collective-permute-start(f32[32,4,256]{2,1,0:T(4,128)S(1)} %get-tuple-element.622), channel_id=1, source_target_pairs={{4,0},{8,4},{12,8},{5,1},{9,5},{13,9},{6,2},{10,6},{14,10},{7,3},{... | collective-permute-start | bytes 393224 | tf_op jit(solution)/shard_map/while/body/eval_jaxpr/ppermute | solution.py:22
  414.8 5.6 collective-permute-start.2
  435.6 7.0 %collective-permute-start.5 = (f32[32,4,256]{2,1,0:T(4,128)S(1)}, f32[32,4,256]{2,1,0:T(4,128)S(1)}, u32[]{:S(2)}, u32[]{:S(2)}) collective-permute-start(f32[32,4,256]{2,1,0:T(4,128)S(1)} %get-tuple-element.625), channel_id=1, source_target_pairs={{4,0},{8,4},{12,8},{5,1},{9,5},{13,9},{6,2},{10,6},{14,10},{7,3},{... | collective-permute-start | bytes 393224 | tf_op jit(solution)/shard_map/while/body/eval_jaxpr/ppermute | solution.py:22
  438.2 6.3 %collective-permute-start.4 = (f32[32,4,256]{2,1,0:T(4,128)S(1)}, f32[32,4,256]{2,1,0:T(4,128)S(1)}, u32[]{:S(2)}, u32[]{:S(2)}) collective-permute-start(f32[32,4,256]{2,1,0:T(4,128)S(1)} %get-tuple-element.624), channel_id=1, source_target_pairs={{0,4},{4,8},{8,12},{1,5},{5,9},{9,13},{2,6},{6,10},{10,14},{3,7},{... | collective-permute-start | bytes 393224 | tf_op jit(solution)/shard_map/while/body/eval_jaxpr/ppermute | solution.py:20
  459.8 15.0 %collective-permute-start.7 = (f32[32,4,256]{2,1,0:T(4,128)S(1)}, f32[32,4,256]{2,1,0:T(4,128)S(1)}, u32[]{:S(2)}, u32[]{:S(2)}) collective-permute-start(f32[32,4,256]{2,1,0:T(4,128)S(1)} %get-tuple-element.628), channel_id=1, source_target_pairs={{4,0},{8,4},{12,8},{5,1},{9,5},{13,9},{6,2},{10,6},{14,10},{7,3},{... | collective-permute-start | bytes 393224 | tf_op jit(solution)/shard_map/while/body/eval_jaxpr/ppermute | solution.py:22
  470.5 6.3 %collective-permute-start.6 = (f32[32,4,256]{2,1,0:T(4,128)S(1)}, f32[32,4,256]{2,1,0:T(4,128)S(1)}, u32[]{:S(2)}, u32[]{:S(2)}) collective-permute-start(f32[32,4,256]{2,1,0:T(4,128)S(1)} %get-tuple-element.627), channel_id=1, source_target_pairs={{0,4},{4,8},{8,12},{1,5},{5,9},{9,13},{2,6},{6,10},{10,14},{3,7},{... | collective-permute-start | bytes 393224 | tf_op jit(solution)/shard_map/while/body/eval_jaxpr/ppermute | solution.py:20
  493.8 0.8 copy-start.1
  533.4 1.4 copy-start.2
Sparse Core Ops, SparseCore 0:
  494.7 19.7 reduce-scatter.1
where the time goes:
time: 568 us; the launch traced here: 560 us
  other arithmetic  318 us (56%)
  starting transfers between devices  96.8 us (17%)
  waiting for transfers between devices  42 us (7%)
  loops' own time  34.3 us (6%)
  local copies, waits for them, and re-layouts  25.4 us (4%)
  blocking collectives  17.2 us (3%)
  between operations  13.6 us (2%)
  matrix products  12 us (2%)
    while x32, other arithmetic  239 us
    ppermute x16, starting transfers between devices, with_halo(): lax.ppermute(tail, axis, [(i, (i + 1) % count) for i in range(ends)])  65.4 us
    add x16, other arithmetic, shot_image(): 2.0 * current - previous + courant * laplace_padded(widened)  39.3 us
    another operation x1, loops' own time, per_device(): lax.fori_loop(0, slot_count, shot_image, jnp.zeros((depth_cells, slab_cel...  34.3 us
    ppermute x16, starting transfers between devices, with_halo(): lax.ppermute(head, axis, [((i + 1) % count, i) for i in range(ends)])  31.4 us
    ppermute x16, waiting for transfers between devices, with_halo(): lax.ppermute(tail, axis, [(i, (i + 1) % count) for i in range(ends)])  21.9 us
    reduce_scatter x1, waiting for transfers between devices, per_device(): summed = lax.psum_scatter(gradient, 'shot', scatter_dimension=0, tiled=True)  19.9 us
  transfers between devices with their start and end apart: 33, of which 13 were waited for; matrix products, arithmetic and copies ran while one was open for 3% of the time, Pallas kernels for 0%

commit v1 on v0

v1 whole, which is shorter than its diff:
```python
import functools
import math

import jax
import jax.numpy as jnp
import ml_dtypes
import numpy as np
from jax import lax
from jax.experimental import pallas as pl
from jax.experimental.pallas import tpu as pltpu
from jax.sharding import PartitionSpec as P

stencil_weights = (-205.0 / 72.0, 8.0 / 5.0, -1.0 / 5.0, 8.0 / 315.0, -1.0 / 560.0)
mute_radius = 6.0
MESH = pl.DeviceIdType.MESH
VM = pl.BlockSpec(memory_space=pltpu.VMEM)
SM = pl.BlockSpec(memory_space=pltpu.SMEM)
FULL = lax.Precision.HIGHEST


def two_parts(table):
    table = np.asarray(table, np.float32)
    high = table.astype(ml_dtypes.bfloat16)
    low = (table - high.astype(np.float32)).astype(ml_dtypes.bfloat16)
    return high, low


def difference_table(rows, columns):
    gap = np.abs(np.asarray(rows)[:, None] - np.asarray(columns)[None, :])
    table = np.zeros(gap.shape, np.float64)
    for k in range(1, 5):
        table[gap == k] = stencil_weights[k]
    return table


def across_tables(planes, slab):
    cells = np.arange(slab)
    ghost = np.concatenate([np.arange(-4, 0), np.arange(slab, slab + 4)])
    eye = np.eye(planes)
    return np.concatenate(
        [
            np.kron(eye, difference_table(cells, cells)),
            np.kron(eye, difference_table(cells, ghost)),
        ],
        axis=1,
    )


def fourier_np(length):
    counting = np.arange(length)
    angle = (counting[:, None] * counting[None, :] % length) * (2.0 * math.pi / length)
    return np.cos(angle), np.sin(angle)


def inject_kernel(slab, receivers_ref, residuals_ref, out_ref):
    start = lax.axis_index("block") * slab
    rows = out_ref.shape[2]
    lateral = out_ref.shape[3]
    steps = residuals_ref.shape[1]
    count = receivers_ref.shape[2]
    depth = receivers_ref[0, 0:1, :]
    local = receivers_ref[0, 1:2, :] - start
    side = receivers_ref[0, 2:3, :]
    inside = (local >= 0) & (local < slab)
    place = jnp.where(inside, depth * slab + local, -1)
    row_pick = lax.broadcasted_iota(jnp.int32, (rows, count), 0) == place
    row_pick = jnp.where(row_pick, 1.0, 0.0).astype(jnp.bfloat16)
    side_pick = lax.broadcasted_iota(jnp.int32, (lateral, count), 0) == side
    dims = (((1,), (1,)), ((), ()))
    for t in range(steps):
        value = residuals_ref[0, t : t + 1, :]
        high = value.astype(jnp.bfloat16).astype(jnp.float32)
        low = value - high
        total = lax.dot_general(
            row_pick,
            jnp.where(side_pick, high, 0.0).astype(jnp.bfloat16),
            dims,
            preferred_element_type=jnp.float32,
        )
        total += lax.dot_general(
            row_pick,
            jnp.where(side_pick, low, 0.0).astype(jnp.bfloat16),
            dims,
            preferred_element_type=jnp.float32,
        )
        out_ref[0, t] = total


def inject_all(receivers, residuals, depth_cells, slab, lateral):
    slots, steps, count = residuals.shape
    rows = depth_cells * slab
    return pl.pallas_call(
        functools.partial(inject_kernel, slab),
        grid=(slots,),
        in_specs=[
            pl.BlockSpec((1, 3, count), lambda s: (s, 0, 0)),
            pl.BlockSpec((1, steps, count), lambda s: (s, 0, 0)),
        ],
        out_specs=pl.BlockSpec((1, steps, rows, lateral), lambda s: (s, 0, 0, 0)),
        out_shape=jax.ShapeDtypeStruct((slots, steps, rows, lateral), jnp.float32),
        compiler_params=pltpu.CompilerParams(vmem_limit_bytes=50 * 2**20),
    )(receivers, residuals)


def split_value(value):
    high = value.astype(jnp.bfloat16)
    low = (value - high.astype(jnp.float32)).astype(jnp.bfloat16)
    return high, low


def dot(left, right):
    return jnp.dot(left, right, preferred_element_type=jnp.float32)


def dot_full(left, right):
    return jnp.dot(left, right, preferred_element_type=jnp.float32, precision=FULL)


def step_kernel(
    blocks,
    shots,
    fused,
    steps_ref,
    live_ref,
    courant_ref,
    snaps_ref,
    inj_ref,
    fade_depth_ref,
    fade_flat_ref,
    wx_high_ref,
    wx_low_ref,
    wy_high_ref,
    wy_low_ref,
    *rest,
):
    if fused:
        (mass_ref, spread_ref, ahead_y_ref, back_y_ref, ahead_x_ref, back_x_ref, *rest) = rest
    (out_ref, field, ghost, outgoing, gradient, ghost_send, ghost_recv, *rest) = rest
    slots, step_count = steps_ref.shape
    depth_cells, slab, lateral = courant_ref.shape
    half = depth_cells // 2
    block = lax.axis_index("block")
    shot = lax.axis_index("shot")

    barrier = pltpu.get_barrier_semaphore()

    @pl.when(block > 0)
    def _():
        pl.semaphore_signal(barrier, inc=1, device_id={"block": block - 1}, device_id_type=MESH)

    @pl.when(block < blocks - 1)
    def _():
        pl.semaphore_signal(barrier, inc=1, device_id={"block": block + 1}, device_id_type=MESH)

    if fused:
        (
            mass_all,
            parts,
            total,
            pencil,
            filtered,
            returned,
            mass_sems,
            part_sems,
            pencil_sems,
            return_sems,
        ) = rest
        for off in range(1, blocks):
            peer = lax.rem(block + off, blocks)

            @pl.when((peer != block - 1) & (peer != block + 1))
            def _(peer=peer):
                pl.semaphore_signal(barrier, inc=1, device_id={"block": peer}, device_id_type=MESH)

        for off in range(1, shots):
            peer = lax.rem(shot + off, shots)
            pl.semaphore_signal(barrier, inc=1, device_id={"shot": peer}, device_id_type=MESH)
        pl.semaphore_wait(barrier, blocks - 1 + shots - 1)
    else:

        @pl.when(block > 0)
        def _():
            pl.semaphore_wait(barrier, 1)

        @pl.when(block < blocks - 1)
        def _():
            pl.semaphore_wait(barrier, 1)

    def exchange(sems, axis, size, me, src, dst):
        copies = []
        for off in range(1, size):
            peer = lax.rem(me + off, size)
            copies.append(
                pltpu.make_async_remote_copy(
                    src_ref=src(peer),
                    dst_ref=dst(me),
                    send_sem=sems.at[0, off],
                    recv_sem=sems.at[1, off],
                    device_id={axis: peer},
                    device_id_type=MESH,
                )
            )
        return copies

    if fused:
        mass_copies = exchange(
            mass_sems, "block", blocks, block, lambda p: mass_ref, lambda m: mass_all.at[m]
        )
        for copy in mass_copies:
            copy.start()
        mass_all[block] = mass_ref[...]

    def to_left(t, s):
        return pltpu.make_async_remote_copy(
            src_ref=outgoing.at[t, s, 0],
            dst_ref=ghost.at[t, s, 1],
            send_sem=ghost_send.at[t, s, 0],
            recv_sem=ghost_recv.at[t, s, 1],
            device_id={"block": lax.rem(block + blocks - 1, blocks)},
            device_id_type=MESH,
        )

    def to_right(t, s):
        return pltpu.make_async_remote_copy(
            src_ref=outgoing.at[t, s, 1],
            dst_ref=ghost.at[t, s, 0],
            send_sem=ghost_send.at[t, s, 1],
            recv_sem=ghost_recv.at[t, s, 0],
            device_id={"block": lax.rem(block + 1, blocks)},
            device_id_type=MESH,
        )

    lower = lax.broadcasted_iota(jnp.int32, (half, 8, lateral), 1) < 4

    def swap(value):
        return jnp.concatenate([value[:, 4:8], value[:, 0:4]], axis=1)

    def send_faces(t, s, plane):
        first = field[plane, s, pl.ds(4, half), 0:8, :]
        second = field[plane, s, pl.ds(4 + half, half), 0:8, :]
        outgoing[t, s, 0] = jnp.where(lower, first, swap(second))
        first = field[plane, s, pl.ds(4, half), slab - 8 : slab, :]
        second = field[plane, s, pl.ds(4 + half, half), slab - 8 : slab, :]
        outgoing[t, s, 1] = jnp.where(lower, swap(first), second)

        @pl.when(block > 0)
        def _():
            to_left(t, s).start()

        @pl.when(block < blocks - 1)
        def _():
            to_right(t, s).start()

    def prepare(s, carry):
        edge = jnp.zeros((4, slab, lateral), jnp.float32)
        for plane in range(2):
            field[plane, s, 0:4] = edge
            field[plane, s, depth_cells + 4 : depth_cells + 8] = edge
        field[0, s, 4 : 4 + depth_cells] = inj_ref[s, 0].reshape(depth_cells, slab, lateral)
        field[1, s, 4 : 4 + depth_cells] = jnp.zeros((depth_cells, slab, lateral), jnp.float32)
        send_faces(0, s, 0)
        return carry

    lax.fori_loop(0, slots, prepare, 0)
    gradient[...] = jnp.zeros_like(gradient)

    @pl.when(block == 0)
    def _():
        ghost[:, :, 0] = jnp.zeros((step_count, slots, half, 8, lateral), jnp.float32)

    @pl.when(block == blocks - 1)
    def _():
        ghost[:, :, 1] = jnp.zeros((step_count, slots, half, 8, lateral), jnp.float32)

    def advance(index, carry):
        t = index // slots
        s = lax.rem(index, slots)
        now = lax.rem(t, 2)
        before = 1 - now

        @pl.when(block > 0)
        def _():
            to_right(t, s).wait_recv()

        @pl.when(block < blocks - 1)
        def _():
            to_left(t, s).wait_recv()

        from_left = ghost[t, s, 0]
        from_right = ghost[t, s, 1]
        sides = (
            jnp.where(lower, from_left, swap(from_right)),
            jnp.where(lower, swap(from_left), from_right),
        )
        chosen = steps_ref[s, t]
        live = live_ref[s]
        for c in range(2):
            base = c * half
            centre = field[now, s, 4 + base : 4 + base + half]
            flat = centre.reshape(half * slab, lateral)
            high, low = split_value(flat)
            side_high, side_low = split_value(sides[c].reshape(half * 8, lateral))
            bend = dot(high, wy_high_ref[...])
            bend += dot(low, wy_high_ref[...])
            bend += dot(high, wy_low_ref[...])
            bend += dot(wx_high_ref[...], jnp.concatenate([high, side_high], axis=0))
            bend += dot(wx_high_ref[...], jnp.concatenate([low, side_low], axis=0))
            bend += dot(wx_low_ref[...], jnp.concatenate([high, side_high], axis=0))
            bend = bend.reshape(half, slab, lateral)
            bend += 3.0 * stencil_weights[0] * centre
            for k in range(1, 5):
                up = field[now, s, 4 + base + k : 4 + base + k + half]
                down = field[now, s, 4 + base - k : 4 + base - k + half]
                bend += stencil_weights[k] * (up + down)
            old = field[before, s, 4 + base : 4 + base + half]
            source = inj_ref[s, t + 1, base * slab : (base + half) * slab, :]
            fresh = (
                2.0 * centre
                - old
                + courant_ref[base : base + half] * bend
                + source.reshape(half, slab, lateral)
            )
            field[before, s, 4 + base : 4 + base + half] = fresh
            fade = live - (live * fade_depth_ref[s, base : base + half]) * fade_flat_ref[s][None]
            shown = snaps_ref[s, chosen, base : base + half].astype(jnp.float32)
            gradient[base : base + half] += fade * (fresh * shown)

        @pl.when(t < step_count - 1)
        def _():
            send_faces(t + 1, s, before)

        return carry

    lax.fori_loop(0, step_count * slots, advance, 0)

    def drain(index, carry):
        t = index // slots
        s = lax.rem(index, slots)

        @pl.when(block > 0)
        def _():
            to_left(t, s).wait_send()

        @pl.when(block < blocks - 1)
        def _():
            to_right(t, s).wait_send()

        return carry

    if not fused:
        out_ref[...] = gradient[...]
        lax.fori_loop(0, step_count * slots, drain, 0)
        return

    kept = depth_cells // shots
    owned = kept // blocks
    part_copies = exchange(
        part_sems,
        "shot",
        shots,
        shot,
        lambda p: gradient.at[pl.ds(p * kept, kept)],
        lambda m: parts.at[m],
    )
    for copy in part_copies:
        copy.start()
    lax.fori_loop(0, step_count * slots, drain, 0)
    parts[shot] = gradient[pl.ds(shot * kept, kept)]
    for copy in mass_copies:
        copy.wait()
    wide = mass_all[...].reshape(lateral, mass_all.shape[2])
    scale = lax.dot_general(
        spread_ref[...],
        wide,
        (((1,), (1,)), ((), ())),
        preferred_element_type=jnp.float32,
        precision=FULL,
    )
    for copy in part_copies:
        copy.wait()
    summed = parts[0]
    for i in range(1, shots):
        summed = summed + parts[i]
    total[...] = summed
    pencil_copies = exchange(
        pencil_sems,
        "block",
        blocks,
        block,
        lambda p: total.at[pl.ds(p * owned, owned)],
        lambda m: pencil.at[m],
    )
    for copy in pencil_copies:
        copy.start()
    pencil[block] = total[pl.ds(block * owned, owned)]
    for copy in pencil_copies:
        copy.wait()
    cells = blocks * owned * slab

    def combine(table_ref, pair, sign):
        both = dot_full(table_ref[...], pair)
        real = both[:cells, :lateral] + sign * both[cells:, lateral:]
        imag = both[:cells, lateral:] - sign * both[cells:, :lateral]
        return real, imag

    pair = dot_full(pencil[...].reshape(cells, lateral), ahead_y_ref[...])
    real, imag = combine(ahead_x_ref, pair, 1.0)
    pair = jnp.concatenate([real * scale, imag * scale], axis=1)
    real, imag = combine(back_x_ref, pair, -1.0)
    result = dot_full(jnp.concatenate([real, imag], axis=1), back_y_ref[...])
    filtered[...] = result.reshape(blocks, owned, slab, lateral)
    return_copies = exchange(
        return_sems,
        "block",
        blocks,
        block,
        lambda p: filtered.at[p],
        lambda m: returned.at[m],
    )
    for copy in return_copies:
        copy.start()
    returned[block] = filtered[block]
    for copy in return_copies:
        copy.wait()
    out_ref[...] = returned[...].reshape(kept, slab, lateral)


def run_steps(blocks, shots, fused, operands, out_dims, mass_dims):
    snap_steps, _, courant = operands[:3]
    slots, step_count = snap_steps.shape
    depth_cells, slab, lateral = courant.shape
    half = depth_cells // 2
    dma = pltpu.SemaphoreType.DMA
    scratch = [
        pltpu.VMEM((2, slots, depth_cells + 8, slab, lateral), jnp.float32),
        pltpu.VMEM((step_count, slots, 2, half, 8, lateral), jnp.float32),
        pltpu.VMEM((step_count, slots, 2, half, 8, lateral), jnp.float32),
        pltpu.VMEM((depth_cells, slab, lateral), jnp.float32),
        dma((step_count, slots, 2)),
        dma((step_count, slots, 2)),
    ]
    if fused:
        kept = depth_cells // shots
        owned = kept // blocks
        scratch += [
            pltpu.VMEM((blocks,) + mass_dims, jnp.float32),
            pltpu.VMEM((shots, kept, slab, lateral), jnp.float32),
            pltpu.VMEM((kept, slab, lateral), jnp.float32),
            pltpu.VMEM((blocks, owned, slab, lateral), jnp.float32),
            pltpu.VMEM((blocks, owned, slab, lateral), jnp.float32),
            pltpu.VMEM((blocks, owned, slab, lateral), jnp.float32),
            dma((2, blocks)),
            dma((2, shots)),
            dma((2, blocks)),
            dma((2, blocks)),
        ]
    return pl.pallas_call(
        functools.partial(step_kernel, blocks, shots, fused),
        out_shape=jax.ShapeDtypeStruct(out_dims, jnp.float32),
        in_specs=[SM, SM] + [VM] * (len(operands) - 2),
        out_specs=VM,
        scratch_shapes=scratch,
        compiler_params=pltpu.CompilerParams(
            collective_id=0, has_side_effects=True, vmem_limit_bytes=58 * 2**20
        ),
    )(*operands)


def spectral_tail(gradient, mass_spectrum):
    summed = lax.psum_scatter(gradient, "shot", scatter_dimension=0, tiled=True)
    lateral = summed.shape[2]
    cos_y, sin_y = (jnp.asarray(v, jnp.float32) for v in fourier_np(lateral))
    real = jnp.einsum("zxy,yk->zkx", summed, cos_y, precision=FULL)
    imag = -jnp.einsum("zxy,yk->zkx", summed, sin_y, precision=FULL)
    pencils = lax.all_to_all(
        jnp.stack([real, imag]), "block", split_axis=2, concat_axis=3, tiled=True
    )
    across = pencils.shape[3]
    cos_x, sin_x = (jnp.asarray(v, jnp.float32) for v in fourier_np(across))

    def turn(real, imag, sign):
        first = jnp.einsum("zkx,xa->zka", real, cos_x, precision=FULL)
        first += sign * jnp.einsum("zkx,xa->zka", imag, sin_x, precision=FULL)
        second = jnp.einsum("zkx,xa->zka", imag, cos_x, precision=FULL)
        second -= sign * jnp.einsum("zkx,xa->zka", real, sin_x, precision=FULL)
        return first, second

    real, imag = turn(pencils[0], pencils[1], 1.0)
    real, imag = turn(real * mass_spectrum[None], imag * mass_spectrum[None], -1.0)
    back = lax.all_to_all(
        jnp.stack([real, imag]), "block", split_axis=3, concat_axis=2, tiled=True
    )
    spatial = jnp.einsum("zkx,ky->zxy", back[0], cos_y, precision=FULL)
    spatial -= jnp.einsum("zkx,ky->zxy", back[1], sin_y, precision=FULL)
    return spatial / float(across * lateral)


def per_device(
    courant, snapshots, residuals, receivers, sources, snap_steps, live_counts, mass_spectrum
):
    depth_cells, slab, lateral = courant.shape
    slots = snapshots.shape[0]
    blocks = lax.axis_size("block")
    shots = lax.axis_size("shot")
    half = depth_cells // 2
    kept = depth_cells // shots
    fused = kept % blocks == 0

    injected = inject_all(receivers, residuals, depth_cells, slab, lateral)

    live = (jnp.arange(slots) < live_counts[0]).astype(jnp.float32)
    place = sources.astype(jnp.float32)
    scale = 1.0 / (mute_radius * mute_radius)
    depth_gap = jnp.arange(depth_cells).astype(jnp.float32)[None, :] - place[:, 0:1]
    fade_depth = jnp.broadcast_to(
        jnp.exp(-(depth_gap**2) * scale)[:, :, None, None], (slots, depth_cells, 1, lateral)
    )
    across = lax.axis_index("block") * slab + jnp.arange(slab)
    across_gap = across.astype(jnp.float32)[None, :, None] - place[:, 1][:, None, None]
    side_gap = jnp.arange(lateral).astype(jnp.float32)[None, None, :] - place[:, 2][:, None, None]
    fade_flat = jnp.exp(-(across_gap**2 + side_gap**2) * scale)

    wx_high, wx_low = two_parts(across_tables(half, slab))
    wy_high, wy_low = two_parts(difference_table(np.arange(lateral), np.arange(lateral)))
    operands = [
        snap_steps,
        live,
        courant,
        snapshots,
        injected,
        fade_depth,
        fade_flat,
        jnp.asarray(wx_high),
        jnp.asarray(wx_low),
        jnp.asarray(wy_high),
        jnp.asarray(wy_low),
    ]
    if not fused:
        dims = (depth_cells, slab, lateral)
        return spectral_tail(run_steps(blocks, shots, False, operands, dims, None), mass_spectrum)

    owned = kept // blocks
    wide = blocks * slab
    cos_y, sin_y = fourier_np(lateral)
    cos_x, sin_x = fourier_np(wide)
    cells = owned * wide

    def ordered(table):
        grid = np.zeros((owned, wide, blocks, owned, slab))
        for z in range(owned):
            grid[z, :, :, z, :] = table.reshape(wide, blocks, slab)
        return grid.reshape(cells, cells)

    cos_ahead, sin_ahead = ordered(cos_x), ordered(sin_x)
    lanes = -(-wide // 128) * 128
    spread = np.zeros((owned, wide, lanes))
    for z in range(owned):
        spread[z, :, :wide] = np.eye(wide)
    spread = spread.reshape(cells, lanes) / float(wide * lateral)
    mass = jnp.pad(mass_spectrum, ((0, 0), (0, lanes - wide)))
    tables = [
        spread,
        np.concatenate([cos_y, -sin_y], axis=1),
        np.concatenate([cos_y, -sin_y], axis=0),
        np.concatenate([cos_ahead, sin_ahead], axis=0),
        np.concatenate([cos_ahead.T, sin_ahead.T], axis=0),
    ]
    operands += [mass] + [jnp.asarray(table, jnp.float32) for table in tables]
    return run_steps(blocks, shots, True, operands, (kept, slab, lateral), mass.shape)


def solution(mesh):
    in_specs = (
        P("chain", "block", None),
        P(("chain", "shot"), None, None, "block", None),
        P(("chain", "shot"), None, None),
        P(("chain", "shot"), None, None),
        P(("chain", "shot"), None),
        P(("chain", "shot"), None),
        P(("chain", "shot")),
        P(("chain", "block"), None),
    )
    out_specs = P(("chain", "shot"), "block", None)
    return jax.shard_map(
        per_device, mesh=mesh, in_specs=in_specs, out_specs=out_specs, check_vma=False
    )
```

time: 568 us -> 93 us (0.16); the launches traced: 560 us -> 91.9 us
  other arithmetic: 318 us -> 1.45 us
  starting transfers between devices: 96.8 us -> 0 us
  Pallas kernels: 0 us -> 84.5 us
  waiting for transfers between devices: 42 us -> 0 us
  loops' own time: 34.3 us -> 0 us
  local copies, waits for them, and re-layouts: 25.4 us -> 5.25 us
  blocking collectives: 17.2 us -> 0 us
  between operations: 13.6 us -> 0.7 us
  matrix products: 12 us -> 0 us
    while x32 -> x0, other arithmetic: 239 us -> none
    ppermute x32 -> x0, starting transfers between devices: 96.8 us -> none  [the longest x16 65.4 us: with_halo(): lax.ppermute(tail, axis, [(i, (i + 1) % count) for i in range(ends)])]
    pallas_call x0 -> x2, Pallas kernels: none -> 84.5 us  [the longest x1 60.4 us: run_steps(): pl.pallas_call(functools.partial(step_kernel, blocks, shots, fused), out_...]
    add x24 -> x0, other arithmetic: 46.1 us -> none  [the longest x16 39.3 us: shot_image(): 2.0 * current - previous + courant * laplace_padded(widened)]
    another operation x1 -> x0, loops' own time: 34.3 us -> none  [per_device(): lax.fori_loop(0, slot_count, shot_image, jnp.zeros((depth_cells, slab_cel...]
    ppermute x32 -> x0, waiting for transfers between devices: 22.1 us -> none  [the longest x16 21.9 us: with_halo(): lax.ppermute(tail, axis, [(i, (i + 1) % count) for i in range(ends)])]
    reduce_scatter x1 -> x0, waiting for transfers between devices: 19.9 us -> none  [per_device(): summed = lax.psum_scatter(gradient, 'shot', scatter_dimension=0, tiled=True)]
    all_to_all x2 -> x0, blocking collectives: 17.2 us -> none  [the longest x1 8.76 us: per_device(): lax.all_to_all(jnp.stack([real_lateral, imag_lateral]), 'block', split_ax...]
  transfers between devices with their start and end apart: 33 -> 0, of which waited for: 13 -> 0; matrix products, arithmetic and copies ran while one was open for 3% -> 0% of each run, Pallas kernels for 0% -> 0%
where the time goes in v1:
time: 93 us; the launch traced here: 91.9 us
  Pallas kernels  84.5 us (91%)
  local copies, waits for them, and re-layouts  5.25 us (6%)
  other arithmetic  1.45 us (2%)
    pallas_call x1, Pallas kernels, run_steps(): pl.pallas_call(functools.partial(step_kernel, blocks, shots, fused), out_...  60.4 us
    pallas_call x1, Pallas kernels, inject_all(): pl.pallas_call(functools.partial(inject_kernel, slab), grid=(slots,), in_...  24.1 us
    unnamed x7, local copies, waits for them, and re-layouts  3.56 us

profile of v1, /device:TPU:25, one launch (start us, length us, event | category | flops | bytes accessed | tf_op | source)
XLA Modules:
  0.0 91.9 jit_solution(18047339378433227824)
XLA Ops:
  0.0 0.0 copy-start.1
  0.0 0.0 copy-start
  0.7 0.5 compare_convert_fusion.live_ref
  1.2 1.0 %copy.18.receivers_ref = s32[4,3,2048]{2,1,0:T(4,128)S(1)} copy(s32[4,3,2048]{2,0,1:T(4,128)} %param.20) | data formatting | bytes 196608 | tf_op args[3]
  2.1 1.0 %copy.19.residuals_ref = f32[4,5,2048]{2,1,0:T(8,128)S(1)} copy(f32[4,5,2048]{2,0,1:T(4,128)} %param.19) | data formatting | bytes 327680 | tf_op args[2]
  3.2 24.1 %shard_map.163.inj_ref = f32[4,5,512,256]{3,2,1,0:T(8,128)} custom-call(s32[4,3,2048]{2,1,0:T(4,128)S(1)} %copy.18.receivers_ref, f32[4,5,2048]{2,1,0:T(8,128)S(1)} %copy.19.residuals_ref), custom_call_target="tpu_custom_call" | custom-call | tf_op jit(solution)/shard_map/pallas_call | solution.py:92
  27.2 0.0 copy-done.1
  27.3 0.2 slice_reduce_fusion.1
  27.5 0.1 multiply_exponential_fusion.1
  27.6 0.9 broadcast_in_dim.2.fade_depth_ref
  28.4 0.1 subtract_multiply_fusion
  28.5 0.1 subtract_multiply_fusion.1
  28.6 0.7 multiply_exponential_fusion.fade_flat_ref
  29.3 0.0 copy-done
  29.3 0.6 pad.4.rest_0_
  29.9 60.4 %shard_map.164 = f32[8,16,256]{2,1,0:T(8,128)} custom-call(s32[4,4]{1,0:T(4,128)} %steps_ref.1, f32[4]{0:T(128)} %compare_convert_fusion.live_ref, f32[32,16,256]{2,1,0:T(8,128)} %courant_ref.1, bf16[4,4,32,16,256]{4,3,2,1,0:T(8,128)(2,1)} %snaps_ref.1, f32[4,5,512,256]{3,2,1,0:T(8,128)} %shard_map.163.inj_ref, ...), custom_call_target="tpu_custom_call" | custom-call | tf_op jit(solution)/shard_map/pallas_call | solution.py:457
  90.3 1.6 %copy.22 = f32[8,16,256]{2,1,0:T(8,128)} copy(f32[8,16,256]{2,1,0:T(8,128)} %shard_map.164) | data formatting | bytes 262144
  (4 shorter events, 0.0 us)
Async XLA Ops:
  0.0 27.2 %copy-start.1 = (s32[4,3]{1,0:T(4,128)S(1)}, s32[4,3]{1,0:T(4,128)}, u32[]{:S(2)}) copy-start(s32[4,3]{1,0:T(4,128)} %param.21) | copy-start | bytes 148
  0.0 29.3 %copy-start = (f32[64,64]{1,0:T(8,128)S(1)}, f32[64,64]{1,0:T(8,128)}, u32[]{:S(2)}) copy-start(f32[64,64]{1,0:T(8,128)} %param.24) | copy-start | bytes 49156

commit v2 on v1

v2 whole, which is shorter than its diff:
```python
import functools
import math

import jax
import jax.numpy as jnp
import numpy as np
from jax import lax
from jax.experimental import pallas as pl
from jax.experimental.pallas import tpu as pltpu
from jax.sharding import PartitionSpec as P

stencil_weights = (-205.0 / 72.0, 8.0 / 5.0, -1.0 / 5.0, 8.0 / 315.0, -1.0 / 560.0)
mute_radius = 6.0
MESH = pl.DeviceIdType.MESH
VM = pl.BlockSpec(memory_space=pltpu.VMEM)
SM = pl.BlockSpec(memory_space=pltpu.SMEM)
FULL = lax.Precision.HIGHEST


stencil_unit = 8.0 / 315.0
unit_weights = (None, 63.0, -63.0 / 8.0, 1.0, -9.0 / 128.0)
centre_units = 3.0 * stencil_weights[0] / stencil_unit


def difference_table(rows, columns):
    gap = np.abs(np.asarray(rows)[:, None] - np.asarray(columns)[None, :])
    table = np.zeros(gap.shape, np.float64)
    for k in range(1, 5):
        table[gap == k] = unit_weights[k]
    return table


def plane_tables(planes, slab):
    cells = np.arange(slab)
    ghost = np.concatenate([np.arange(-4, 0), np.arange(slab, slab + 4)])
    depth = np.arange(planes)
    own = np.kron(np.eye(planes), difference_table(cells, cells))
    own += np.kron(difference_table(depth, depth), np.eye(slab))
    sides = np.kron(np.eye(planes), difference_table(cells, ghost))
    tables = []
    for near in (np.arange(planes, planes + 4), np.arange(-4, 0)):
        reach = np.kron(difference_table(depth, near), np.eye(slab))
        spare = np.zeros((planes * slab, 4 * slab))
        one = np.concatenate([own, sides, reach, spare], axis=1)
        tables.append(np.concatenate([one, one], axis=1))
    return np.stack(tables)


def fourier_np(length):
    counting = np.arange(length)
    angle = (counting[:, None] * counting[None, :] % length) * (2.0 * math.pi / length)
    return np.cos(angle), np.sin(angle)


NT = (((1,), (1,)), ((), ()))
GROUP = 128


def inject_kernel(
    slab,
    own_size,
    edge_size,
    receivers_ref,
    residuals_ref,
    sources_ref,
    live_ref,
    tri_ref,
    out_ref,
    ghost_ref,
    fade_ref,
    marks,
    facts,
    ranks,
):
    s = pl.program_id(0)
    start = lax.axis_index("block") * slab
    steps = residuals_ref.shape[0]
    count = receivers_ref.shape[2]
    chunks = count // GROUP
    rows, lateral = out_ref.shape[2:]
    ghost_rows = ghost_ref.shape[1]
    depth_cells = rows // slab

    live = jnp.where(s < live_ref[0], 1.0, 0.0)
    scale = 1.0 / (mute_radius * mute_radius)
    place = [sources_ref[s, i].astype(jnp.float32) for i in range(3)]
    flat = (slab, lateral)
    across = (lax.broadcasted_iota(jnp.int32, flat, 0) + start).astype(jnp.float32) - place[1]
    side = lax.broadcasted_iota(jnp.int32, flat, 1).astype(jnp.float32) - place[2]
    fade_flat = live * jnp.exp(-(across * across + side * side) * scale)
    for z in range(depth_cells):
        gap = jnp.full(flat, z, jnp.float32) - place[0]
        fade_ref[0, z] = live - jnp.exp(-(gap * gap) * scale) * fade_flat

    depth = receivers_ref[0, pl.ds(s, 1), :]
    local = receivers_ref[1, pl.ds(s, 1), :] - start
    lateral_pos = receivers_ref[2, pl.ds(s, 1), :]
    facts[0:1, :] = depth.astype(jnp.float32)
    facts[2:3, :] = (lateral_pos // 16).astype(jnp.float32)
    facts[3:4, :] = lax.rem(lateral_pos, 16).astype(jnp.float32)
    for t in range(steps):
        value = residuals_ref[t, pl.ds(s, 1), :]
        high = value.astype(jnp.bfloat16).astype(jnp.float32)
        facts[4 + 2 * t : 5 + 2 * t, :] = high
        facts[5 + 2 * t : 6 + 2 * t, :] = value - high
    used = 4 + 2 * steps
    facts[used:, :] = jnp.zeros((facts.shape[0] - used, count), jnp.float32)

    def rank(inside):
        flag = jnp.where(inside, 1.0, 0.0)
        for c in range(chunks):
            marks[c : c + 1, :] = flag[:, c * GROUP : (c + 1) * GROUP]
        mark = marks[...]
        through = jnp.dot(
            mark.astype(jnp.bfloat16), tri_ref[...], preferred_element_type=jnp.float32
        )
        total = jnp.zeros((1, 1), jnp.float32)
        for c in range(chunks):
            ranks[c : c + 1, :] = jnp.where(
                mark[c : c + 1] > 0.0, through[c : c + 1] + (total - 1.0), -1.0
            ).astype(jnp.int32)
            total = total + through[c : c + 1, GROUP - 1 :]
        return jnp.sum(flag).astype(jnp.int32)

    def gather(first, size):
        slot = lax.broadcasted_iota(jnp.int32, (size, GROUP), 0) + first
        pick = jnp.concatenate(
            [
                jnp.where(slot == ranks[c : c + 1, :], 1.0, 0.0).astype(jnp.bfloat16)
                for c in range(chunks)
            ],
            axis=1,
        )
        return lax.dot_general(
            facts[...].astype(jnp.bfloat16), pick, NT, preferred_element_type=jnp.float32
        )

    def spread(found, width, row_count, t_list):
        where = found[0:1] * float(width) + found[1:2]
        size = found.shape[1]
        row = lax.broadcasted_iota(jnp.int32, (row_count, size), 0)
        row = jnp.where(row == where.astype(jnp.int32), 1.0, 0.0).astype(jnp.bfloat16)
        row = jnp.concatenate([row, row], axis=1)
        lane = (found[2:3] * 16.0 + found[3:4]).astype(jnp.int32)
        hit = lax.broadcasted_iota(jnp.int32, (lateral, size), 0) == lane
        for t in t_list:
            pair = jnp.concatenate(
                [
                    jnp.where(hit, found[4 + 2 * t + i : 5 + 2 * t + i], 0.0).astype(jnp.bfloat16)
                    for i in range(2)
                ],
                axis=1,
            )
            yield t, lax.dot_general(row, pair, NT, preferred_element_type=jnp.float32)

    inside = (local >= 0) & (local < slab)
    facts[1:2, :] = jnp.where(inside, local, 0).astype(jnp.float32)
    own_total = rank(inside)
    for t, value in spread(gather(0, own_size), slab, rows, range(steps)):
        out_ref[0, t] = value

    def own_group(group, carry):
        for t, add in spread(gather(own_size + group * GROUP, GROUP), slab, rows, range(steps)):
            out_ref[0, t] += add
        return carry

    lax.fori_loop(0, jnp.maximum(own_total - own_size + GROUP - 1, 0) // GROUP, own_group, 0)

    left = (local >= -4) & (local < 0)
    right = (local >= slab) & (local < slab + 4)
    column = jnp.where(left, local + 4, jnp.where(right, local - slab + 4, 0))
    facts[1:2, :] = column.astype(jnp.float32)
    edge_total = rank(left | right)
    for _, value in spread(gather(0, edge_size), 8, ghost_rows, (0,)):
        ghost_ref[0] = value

    def ghost_group(group, carry):
        for _, add in spread(gather(edge_size + group * GROUP, GROUP), 8, ghost_rows, (0,)):
            ghost_ref[0] += add
        return carry

    lax.fori_loop(0, jnp.maximum(edge_total - edge_size + GROUP - 1, 0) // GROUP, ghost_group, 0)


def inject_all(receivers, residuals, sources, live_counts, depth_cells, slab, lateral):
    steps, slots, count = residuals.shape
    rows = depth_cells * slab
    ghost_rows = depth_cells * 8
    blocks = lax.axis_size("block")
    own_size = min(count, (-(-count // blocks // GROUP) + 1) * GROUP)
    edge_size = min(count, (-(-8 * count // (blocks * slab) // GROUP) + 1) * GROUP)
    tri = jnp.asarray(np.triu(np.ones((GROUP, GROUP))), jnp.bfloat16)
    fact_rows = -(-(4 + 2 * steps) // 16) * 16
    return pl.pallas_call(
        functools.partial(inject_kernel, slab, own_size, edge_size),
        grid=(slots,),
        in_specs=[VM, VM, SM, SM, VM],
        out_specs=[
            pl.BlockSpec((1, steps, rows, lateral), lambda s: (s, 0, 0, 0)),
            pl.BlockSpec((1, ghost_rows, lateral), lambda s: (s, 0, 0)),
            pl.BlockSpec((1, depth_cells, slab, lateral), lambda s: (s, 0, 0, 0)),
        ],
        out_shape=[
            jax.ShapeDtypeStruct((slots, steps, rows, lateral), jnp.float32),
            jax.ShapeDtypeStruct((slots, ghost_rows, lateral), jnp.float32),
            jax.ShapeDtypeStruct((slots, depth_cells, slab, lateral), jnp.float32),
        ],
        scratch_shapes=[
            pltpu.VMEM((count // GROUP, GROUP), jnp.float32),
            pltpu.VMEM((fact_rows, count), jnp.float32),
            pltpu.VMEM((count // GROUP, GROUP), jnp.int32),
        ],
        compiler_params=pltpu.CompilerParams(vmem_limit_bytes=62 * 2**20),
    )(receivers, residuals, sources, live_counts, tri)


def split_value(value):
    high = value.astype(jnp.bfloat16)
    low = (value - high.astype(jnp.float32)).astype(jnp.bfloat16)
    return high, low


def dot(left, right):
    return jnp.dot(left, right, preferred_element_type=jnp.float32)


def dot_full(left, right):
    return jnp.dot(left, right, preferred_element_type=jnp.float32, precision=FULL)


def step_kernel(blocks, shots, fused, late, *refs):
    steps_ref, courant_ref, plane_ref, lateral_ref, *rest = refs
    stored = rest[:late]
    if fused:
        mass_ref = rest[late]
        rest = rest[1:]
    out_ref, *rest = rest[late:]
    local = rest[:late]
    (load_sems, field, highs, lows, scaled, gradient, ghost, outgoing, ghost_sems, *rest) = rest[
        late:
    ]
    inj_ref, edge_ref, snaps_ref, fade_ref = local[:4]
    slots, step_count = steps_ref.shape
    depth_cells, slab, lateral = courant_ref.shape
    half = depth_cells // 2
    block = lax.axis_index("block")
    shot = lax.axis_index("shot")

    def load(i, s):
        return pltpu.make_async_copy(stored[i].at[s], local[i].at[s], load_sems.at[i, s])

    def load_table(i):
        return pltpu.make_async_copy(stored[i], local[i], load_sems.at[i, 0])

    for s in range(slots):
        for i in range(4):
            load(i, s).start()
    for i in range(4, late):
        load_table(i).start()

    barrier = pltpu.get_barrier_semaphore()

    @pl.when(block > 0)
    def _():
        pl.semaphore_signal(barrier, inc=1, device_id={"block": block - 1}, device_id_type=MESH)

    @pl.when(block < blocks - 1)
    def _():
        pl.semaphore_signal(barrier, inc=1, device_id={"block": block + 1}, device_id_type=MESH)

    if fused:
        (
            mass_own,
            mass_all,
            parts,
            total,
            pencil,
            filtered,
            returned,
            mass_sems,
            part_sems,
            pencil_sems,
            return_sems,
        ) = rest
        for off in range(1, blocks):
            peer = lax.rem(block + off, blocks)

            @pl.when((peer != block - 1) & (peer != block + 1))
            def _(peer=peer):
                pl.semaphore_signal(barrier, inc=1, device_id={"block": peer}, device_id_type=MESH)

        for off in range(1, shots):
            peer = lax.rem(shot + off, shots)
            pl.semaphore_signal(barrier, inc=1, device_id={"shot": peer}, device_id_type=MESH)
        mass_own[...] = jnp.zeros_like(mass_own)
        mass_own[:, 0 : mass_ref.shape[1]] = mass_ref[...]
    gradient[...] = jnp.zeros_like(gradient)
    scaled[...] = courant_ref[...] * stencil_unit

    @pl.when(block == 0)
    def _():
        ghost[:, :, 0] = jnp.zeros((step_count - 1, slots, half, 8, lateral), jnp.float32)

    @pl.when(block == blocks - 1)
    def _():
        ghost[:, :, 1] = jnp.zeros((step_count - 1, slots, half, 8, lateral), jnp.float32)

    if fused:
        pl.semaphore_wait(barrier, blocks - 1 + shots - 1)
    else:

        @pl.when(block > 0)
        def _():
            pl.semaphore_wait(barrier, 1)

        @pl.when(block < blocks - 1)
        def _():
            pl.semaphore_wait(barrier, 1)

    def exchange(sems, axis, size, me, src, dst):
        copies = []
        for off in range(1, size):
            peer = lax.rem(me + off, size)
            copies.append(
                pltpu.make_async_remote_copy(
                    src_ref=src(peer),
                    dst_ref=dst(me),
                    send_sem=sems.at[0, off],
                    recv_sem=sems.at[1, off],
                    device_id={axis: peer},
                    device_id_type=MESH,
                )
            )
        return copies

    if fused:
        mass_copies = exchange(
            mass_sems, "block", blocks, block, lambda p: mass_own, lambda m: mass_all.at[m]
        )
        for copy in mass_copies:
            copy.start()
        mass_all[block] = mass_own[...]

    def to_left(t, s):
        return pltpu.make_async_remote_copy(
            src_ref=outgoing.at[t, s, 0],
            dst_ref=ghost.at[t, s, 1],
            send_sem=ghost_sems.at[0, t, s, 0],
            recv_sem=ghost_sems.at[1, t, s, 1],
            device_id={"block": lax.rem(block + blocks - 1, blocks)},
            device_id_type=MESH,
        )

    def to_right(t, s):
        return pltpu.make_async_remote_copy(
            src_ref=outgoing.at[t, s, 1],
            dst_ref=ghost.at[t, s, 0],
            send_sem=ghost_sems.at[0, t, s, 1],
            recv_sem=ghost_sems.at[1, t, s, 0],
            device_id={"block": lax.rem(block + 1, blocks)},
            device_id_type=MESH,
        )

    lower = lax.broadcasted_iota(jnp.int32, (half, 8, lateral), 1) < 4

    def swap(value):
        return jnp.concatenate([value[:, 4:8], value[:, 0:4]], axis=1)

    def send_faces(t, s, plane):
        first = field[plane, s, 0:half, 0:8, :]
        second = field[plane, s, half:depth_cells, 0:8, :]
        outgoing[t, s, 0] = jnp.where(lower, first, swap(second))
        first = field[plane, s, 0:half, slab - 8 : slab, :]
        second = field[plane, s, half:depth_cells, slab - 8 : slab, :]
        outgoing[t, s, 1] = jnp.where(lower, swap(first), second)

        @pl.when(block > 0)
        def _():
            to_left(t, s).start()

        @pl.when(block < blocks - 1)
        def _():
            to_right(t, s).start()

    spare = jnp.zeros((4 * slab, lateral), jnp.bfloat16)
    rows = half * slab

    def bend(t, s, c, tile):
        now = t % 2
        near = slice(rows, rows + 4 * slab) if c == 0 else slice(rows - 4 * slab, rows)
        here = slice(c * rows, (c + 1) * rows)
        stack = []
        if t == 0:
            own = split_value(inj_ref[s, 0, here])
            reach = split_value(inj_ref[s, 0, near])
        else:
            own = (highs[now, s, here], lows[now, s, here])
            reach = (highs[now, s, near], lows[now, s, near])
        side = split_value(tile)
        for i in range(2):
            stack += [own[i], side[i], reach[i], spare]
        result = dot(plane_ref[c], jnp.concatenate(stack, axis=0))
        return result + dot(jnp.concatenate(own, axis=1), lateral_ref[...])

    def update(t, s, c, sums):
        now, later = t % 2, (t + 1) % 2
        chosen = steps_ref[s, t]
        for z in range(half):
            depth = c * half + z
            span = slice(depth * slab, (depth + 1) * slab)
            centre = inj_ref[s, 0, span] if t == 0 else field[now, s, depth]
            fresh = 2.0 * centre + inj_ref[s, t + 1, span]
            if t == 1:
                fresh -= inj_ref[s, 0, span]
            elif t > 1:
                fresh -= field[later, s, depth]
            fresh += scaled[depth] * (sums[z * slab : (z + 1) * slab] + centre_units * centre)
            if t < step_count - 1:
                field[later, s, depth] = fresh
                highs[later, s, span], lows[later, s, span] = split_value(fresh)
            shown = snaps_ref[s, chosen, depth].astype(jnp.float32)
            gradient[depth] += fade_ref[s, depth] * (fresh * shown)

    def tiles(t, s):
        if t == 0:
            return [edge_ref[s, c * half * 8 : (c + 1) * half * 8] for c in range(2)]

        from_left = ghost[t - 1, s, 0]
        from_right = ghost[t - 1, s, 1]
        return [
            jnp.where(lower, from_left, swap(from_right)).reshape(half * 8, lateral),
            jnp.where(lower, swap(from_left), from_right).reshape(half * 8, lateral),
        ]

    def arrive(t, s):
        if t == 0:
            for i in (0, 1, 3):
                load(i, s).wait()
            return

        @pl.when(block > 0)
        def _():
            to_right(t - 1, s).wait_recv()

        @pl.when(block < blocks - 1)
        def _():
            to_left(t - 1, s).wait_recv()

    for s in range(slots):
        load(2, s).wait()

    for t in range(step_count - 1):

        def advance(s, carry, t=t):
            arrive(t, s)
            tile = tiles(t, s)
            sums = [bend(t, s, c, tile[c]) for c in range(2)]
            for c in range(2):
                update(t, s, c, sums[c])
            send_faces(t, s, (t + 1) % 2)
            return carry

        lax.fori_loop(0, slots, advance, 0)

    if fused:
        kept = depth_cells // shots
        owned = kept // blocks
        part_copies = exchange(
            part_sems,
            "shot",
            shots,
            shot,
            lambda p: gradient.at[pl.ds(p * kept, kept)],
            lambda m: parts.at[m],
        )
    t = step_count - 1
    for c in range(2):

        def finish(s, carry, c=c):
            if c == 0:
                arrive(t, s)
            update(t, s, c, bend(t, s, c, tiles(t, s)[c]))
            return carry

        lax.fori_loop(0, slots, finish, 0)
        if fused:
            for off in range(1, shots):
                peer = lax.rem(shot + off, shots)

                @pl.when((peer * kept >= c * half) & (peer * kept < (c + 1) * half))
                def _(off=off):
                    part_copies[off - 1].start()

    def drain(index, carry):
        t = index // slots
        s = lax.rem(index, slots)

        @pl.when(block > 0)
        def _():
            to_left(t, s).wait_send()

        @pl.when(block < blocks - 1)
        def _():
            to_right(t, s).wait_send()

        return carry

    lax.fori_loop(0, (step_count - 1) * slots, drain, 0)
    if not fused:
        out_ref[...] = gradient[...]
        return

    for i in range(4, late):
        load_table(i).wait()
    spread_ref, ahead_y_ref, back_y_ref, ahead_x_ref, back_x_ref = local[4:]
    parts[shot] = gradient[pl.ds(shot * kept, kept)]
    for copy in mass_copies:
        copy.wait()
    wide = mass_all[...].reshape(lateral, mass_all.shape[2])
    scale = lax.dot_general(
        spread_ref[...], wide, NT, preferred_element_type=jnp.float32, precision=FULL
    )
    for copy in part_copies:
        copy.wait()
    summed = parts[0]
    for i in range(1, shots):
        summed = summed + parts[i]
    total[...] = summed
    pencil_copies = exchange(
        pencil_sems,
        "block",
        blocks,
        block,
        lambda p: total.at[pl.ds(p * owned, owned)],
        lambda m: pencil.at[m],
    )
    for copy in pencil_copies:
        copy.start()
    pencil[block] = total[pl.ds(block * owned, owned)]
    for copy in pencil_copies:
        copy.wait()
    cells = blocks * owned * slab

    def combine(table_ref, pair, sign):
        both = dot_full(table_ref[...], pair)
        real = both[:cells, :lateral] + sign * both[cells:, lateral:]
        imag = both[:cells, lateral:] - sign * both[cells:, :lateral]
        return real, imag

    pair = dot_full(pencil[...].reshape(cells, lateral), ahead_y_ref[...])
    real, imag = combine(ahead_x_ref, pair, 1.0)
    pair = jnp.concatenate([real * scale, imag * scale], axis=1)
    real, imag = combine(back_x_ref, pair, -1.0)
    result = dot_full(jnp.concatenate([real, imag], axis=1), back_y_ref[...])
    filtered[...] = result.reshape(blocks, owned, slab, lateral)
    return_copies = exchange(
        return_sems,
        "block",
        blocks,
        block,
        lambda p: filtered.at[p],
        lambda m: returned.at[m],
    )
    for copy in return_copies:
        copy.start()
    returned[block] = filtered[block]
    for copy in return_copies:
        copy.wait()
    out_ref[...] = returned[...].reshape(kept, slab, lateral)


def run_steps(blocks, shots, fused, direct, stored, mass, out_dims):
    snap_steps, courant = direct[:2]
    slots, step_count = snap_steps.shape
    depth_cells, slab, lateral = courant.shape
    half = depth_cells // 2
    dma = pltpu.SemaphoreType.DMA
    cube = (depth_cells, slab, lateral)
    scratch = [pltpu.VMEM(array.shape, array.dtype) for array in stored]
    scratch += [
        dma((len(stored), slots)),
        pltpu.VMEM((2, slots) + cube, jnp.float32),
        pltpu.VMEM((2, slots, depth_cells * slab, lateral), jnp.bfloat16),
        pltpu.VMEM((2, slots, depth_cells * slab, lateral), jnp.bfloat16),
        pltpu.VMEM(cube, jnp.float32),
        pltpu.VMEM(cube, jnp.float32),
        pltpu.VMEM((step_count - 1, slots, 2, half, 8, lateral), jnp.float32),
        pltpu.VMEM((step_count - 1, slots, 2, half, 8, lateral), jnp.float32),
        dma((2, step_count - 1, slots, 2)),
    ]
    operands = list(direct) + list(stored)
    specs = [SM] + [VM] * (len(direct) - 1) + [pl.BlockSpec(memory_space=pltpu.HBM)] * len(stored)
    if fused:
        operands.append(mass)
        specs.append(VM)
        kept = depth_cells // shots
        owned = kept // blocks
        lanes = stored[4].shape[1]
        scratch += [
            pltpu.VMEM((mass.shape[0], lanes), jnp.float32),
            pltpu.VMEM((blocks, mass.shape[0], lanes), jnp.float32),
            pltpu.VMEM((shots, kept, slab, lateral), jnp.float32),
            pltpu.VMEM((kept, slab, lateral), jnp.float32),
            pltpu.VMEM((blocks, owned, slab, lateral), jnp.float32),
            pltpu.VMEM((blocks, owned, slab, lateral), jnp.float32),
            pltpu.VMEM((blocks, owned, slab, lateral), jnp.float32),
            dma((2, blocks)),
            dma((2, shots)),
            dma((2, blocks)),
            dma((2, blocks)),
        ]
    return pl.pallas_call(
        functools.partial(step_kernel, blocks, shots, fused, len(stored)),
        out_shape=jax.ShapeDtypeStruct(out_dims, jnp.float32),
        in_specs=specs,
        out_specs=VM,
        scratch_shapes=scratch,
        compiler_params=pltpu.CompilerParams(
            collective_id=0, has_side_effects=True, vmem_limit_bytes=58 * 2**20
        ),
    )(*operands)


def spectral_tail(gradient, mass_spectrum):
    summed = lax.psum_scatter(gradient, "shot", scatter_dimension=0, tiled=True)
    lateral = summed.shape[2]
    cos_y, sin_y = (jnp.asarray(v, jnp.float32) for v in fourier_np(lateral))
    real = jnp.einsum("zxy,yk->zkx", summed, cos_y, precision=FULL)
    imag = -jnp.einsum("zxy,yk->zkx", summed, sin_y, precision=FULL)
    pencils = lax.all_to_all(
        jnp.stack([real, imag]), "block", split_axis=2, concat_axis=3, tiled=True
    )
    across = pencils.shape[3]
    cos_x, sin_x = (jnp.asarray(v, jnp.float32) for v in fourier_np(across))

    def turn(real, imag, sign):
        first = jnp.einsum("zkx,xa->zka", real, cos_x, precision=FULL)
        first += sign * jnp.einsum("zkx,xa->zka", imag, sin_x, precision=FULL)
        second = jnp.einsum("zkx,xa->zka", imag, cos_x, precision=FULL)
        second -= sign * jnp.einsum("zkx,xa->zka", real, sin_x, precision=FULL)
        return first, second

    real, imag = turn(pencils[0], pencils[1], 1.0)
    real, imag = turn(real * mass_spectrum[None], imag * mass_spectrum[None], -1.0)
    back = lax.all_to_all(
        jnp.stack([real, imag]), "block", split_axis=3, concat_axis=2, tiled=True
    )
    spatial = jnp.einsum("zkx,ky->zxy", back[0], cos_y, precision=FULL)
    spatial -= jnp.einsum("zkx,ky->zxy", back[1], sin_y, precision=FULL)
    return spatial / float(across * lateral)


def per_device(
    courant, snapshots, residuals, receivers, sources, snap_steps, live_counts, mass_spectrum
):
    depth_cells, slab, lateral = courant.shape
    blocks = lax.axis_size("block")
    shots = lax.axis_size("shot")
    half = depth_cells // 2
    kept = depth_cells // shots
    fused = kept % blocks == 0

    injected, edges, fade = inject_all(
        jnp.transpose(receivers, (1, 0, 2)),
        jnp.transpose(residuals, (1, 0, 2)),
        sources,
        live_counts,
        depth_cells,
        slab,
        lateral,
    )
    lateral_table = difference_table(np.arange(lateral), np.arange(lateral))
    direct = [
        snap_steps,
        courant,
        jnp.asarray(plane_tables(half, slab), jnp.bfloat16),
        jnp.asarray(np.concatenate([lateral_table] * 2, axis=0), jnp.bfloat16),
    ]
    stored = [injected, edges, snapshots, fade]
    if not fused:
        dims = (depth_cells, slab, lateral)
        summed = run_steps(blocks, shots, False, direct, stored, None, dims)
        return spectral_tail(summed, mass_spectrum)

    owned = kept // blocks
    wide = blocks * slab
    cos_y, sin_y = fourier_np(lateral)
    cos_x, sin_x = fourier_np(wide)
    cells = owned * wide

    def ordered(table):
        grid = np.zeros((owned, wide, blocks, owned, slab))
        for z in range(owned):
            grid[z, :, :, z, :] = table.reshape(wide, blocks, slab)
        return grid.reshape(cells, cells)

    cos_ahead, sin_ahead = ordered(cos_x), ordered(sin_x)
    lanes = -(-wide // 128) * 128
    spread = np.zeros((owned, wide, lanes))
    for z in range(owned):
        spread[z, :, :wide] = np.eye(wide)
    spread = spread.reshape(cells, lanes) / float(wide * lateral)
    tables = [
        spread,
        np.concatenate([cos_y, -sin_y], axis=1),
        np.concatenate([cos_y, -sin_y], axis=0),
        np.concatenate([cos_ahead, sin_ahead], axis=0),
        np.concatenate([cos_ahead.T, sin_ahead.T], axis=0),
    ]
    stored += [jnp.asarray(table, jnp.float32) for table in tables]
    return run_steps(
        blocks, shots, True, direct, stored, mass_spectrum, (kept, slab, lateral)
    )


def solution(mesh):
    in_specs = (
        P("chain", "block", None),
        P(("chain", "shot"), None, None, "block", None),
        P(("chain", "shot"), None, None),
        P(("chain", "shot"), None, None),
        P(("chain", "shot"), None),
        P(("chain", "shot"), None),
        P(("chain", "shot")),
        P(("chain", "block"), None),
    )
    out_specs = P(("chain", "shot"), "block", None)
    return jax.shard_map(
        per_device, mesh=mesh, in_specs=in_specs, out_specs=out_specs, check_vma=False
    )
```

time: 93 us -> 72.1 us (0.78); the launches traced: 91.9 us -> 71.9 us
  Pallas kernels: 84.5 us -> 69.7 us
  local copies, waits for them, and re-layouts: 5.25 us -> 1.57 us
  other arithmetic: 1.45 us -> 0 us
    pallas_call x2, Pallas kernels: 84.5 us -> 69.7 us  [the longest x1 49.2 us: run_steps(): pl.pallas_call(functools.partial(step_kernel, blocks, shots, fused, len(s...]
    unnamed x7 -> x1, local copies, waits for them, and re-layouts: 3.56 us -> 1.57 us
where the time goes in v2:
time: 72.1 us; the launch traced here: 71.9 us
  Pallas kernels  69.7 us (97%)
  local copies, waits for them, and re-layouts  1.57 us (2%)
    pallas_call x1, Pallas kernels, run_steps(): pl.pallas_call(functools.partial(step_kernel, blocks, shots, fused, len(s...  49.2 us
    pallas_call x1, Pallas kernels, inject_all(): pl.pallas_call(functools.partial(inject_kernel, slab, own_size, edge_size...  20.5 us
    unnamed x1, local copies, waits for them, and re-layouts  1.57 us

profile of v2, /device:TPU:25, one launch (start us, length us, event | category | flops | bytes accessed | tf_op | source)
XLA Modules:
  0.0 71.9 jit_solution(2804873354885110223)
XLA Ops:
  0.7 20.5 %shard_map.154 = (f32[4,5,512,256]{3,2,1,0:T(8,128)}, f32[4,256,256]{2,1,0:T(8,128)}, f32[4,32,16,256]{3,2,1,0:T(8,128)}) custom-call(s32[3,4,2048]{2,1,0:T(4,128)} %bitcast.3, f32[5,4,2048]{2,1,0:T(4,128)} %bitcast.2, s32[4,3]{1,0:T(4,128)} %sources_ref.1, s32[1]{0:T(128)S(6)} %copy.18.live_ref, bf16[128,128]{1,0:T(8,128)(2,1)} %constant.16.clone.tri_ref), custom_call_target="tpu_custom_call" | custom-call | tf_op jit(solution)/shard_map/pallas_call | solution.py:194
  21.1 49.2 %shard_map.155 = f32[8,16,256]{2,1,0:T(8,128)} custom-call(s32[4,4]{1,0:T(4,128)} %refs_0_.1, f32[32,16,256]{2,1,0:T(8,128)} %refs_1_.1, bf16[2,256,1024]{2,1,0:T(8,128)(2,1)} %constant.17.clone.refs_2_, bf16[512,256]{1,0:T(8,128)(2,1)} %constant.18.clone.refs_3_, f32[4,5,512,256]{3,2,1,0:T(8,128)} %get-tuple-element.8.refs_4_, ...), custom_call_target="tpu_custom_call" | custom-call | tf_op jit(solution)/shard_map/pallas_call | solution.py:612
  70.4 1.6 %copy.19 = f32[8,16,256]{2,1,0:T(8,128)} copy(f32[8,16,256]{2,1,0:T(8,128)} %shard_map.155) | data formatting | bytes 262144

commit v3 on v2

--- a/solution.py
+++ b/solution.py
@@ -3,6 +3,7 @@
 
 import jax
 import jax.numpy as jnp
+import ml_dtypes
 import numpy as np
 from jax import lax
 from jax.experimental import pallas as pl
@@ -15,6 +16,11 @@
 VM = pl.BlockSpec(memory_space=pltpu.VMEM)
 SM = pl.BlockSpec(memory_space=pltpu.SMEM)
 FULL = lax.Precision.HIGHEST
+
+
+def two_parts(table):
+    high = table.astype(ml_dtypes.bfloat16)
+    return np.stack([high, (table - high.astype(np.float64)).astype(ml_dtypes.bfloat16)])
 
 
 stencil_unit = 8.0 / 315.0
@@ -224,8 +230,14 @@
     return jnp.dot(left, right, preferred_element_type=jnp.float32)
 
 
-def dot_full(left, right):
-    return jnp.dot(left, right, preferred_element_type=jnp.float32, precision=FULL)
+def dot_right(value, table_ref):
+    high, low = split_value(value)
+    return dot(high, table_ref[0]) + (dot(low, table_ref[0]) + dot(high, table_ref[1]))
+
+
+def dot_left(table_ref, value):
+    high, low = split_value(value)
+    return dot(table_ref[0], high) + (dot(table_ref[0], low) + dot(table_ref[1], high))
 
 
 def step_kernel(blocks, shots, fused, late, *refs):
@@ -247,14 +259,25 @@
     shot = lax.axis_index("shot")
 
     def load(i, s):
+        if i == 0:
+            span = (s, slice(0, 2))
+            return pltpu.make_async_copy(stored[0].at[span], local[0].at[span], load_sems.at[0, s])
         return pltpu.make_async_copy(stored[i].at[s], local[i].at[s], load_sems.at[i, s])
+
+    def load_later(s):
+        span = (s, slice(2, steps_ref.shape[1] + 1))
+        return pltpu.make_async_copy(stored[0].at[span], local[0].at[span], load_sems.at[late, s])
 
     def load_table(i):
         return pltpu.make_async_copy(stored[i], local[i], load_sems.at[i, 0])
 
     for s in range(slots):
-        for i in range(4):
+        load(2, s).start()
+    for s in range(slots):
+        for i in (0, 1, 3):
             load(i, s).start()
+    for s in range(slots):
+        load_later(s).start()
     for i in range(4, late):
         load_table(i).start()
 
@@ -437,6 +460,8 @@
             for i in (0, 1, 3):
                 load(i, s).wait()
             return
+        if t == 1:
+            load_later(s).wait()
 
         @pl.when(block > 0)
         def _():
@@ -542,16 +567,16 @@
     cells = blocks * owned * slab
 
     def combine(table_ref, pair, sign):
-        both = dot_full(table_ref[...], pair)
+        both = dot_left(table_ref, pair)
         real = both[:cells, :lateral] + sign * both[cells:, lateral:]
         imag = both[:cells, lateral:] - sign * both[cells:, :lateral]
         return real, imag
 
-    pair = dot_full(pencil[...].reshape(cells, lateral), ahead_y_ref[...])
+    pair = dot_right(pencil[...].reshape(cells, lateral), ahead_y_ref)
     real, imag = combine(ahead_x_ref, pair, 1.0)
     pair = jnp.concatenate([real * scale, imag * scale], axis=1)
     real, imag = combine(back_x_ref, pair, -1.0)
-    result = dot_full(jnp.concatenate([real, imag], axis=1), back_y_ref[...])
+    result = dot_right(jnp.concatenate([real, imag], axis=1), back_y_ref)
     filtered[...] = result.reshape(blocks, owned, slab, lateral)
     return_copies = exchange(
         return_sems,
@@ -578,7 +603,7 @@
     cube = (depth_cells, slab, lateral)
     scratch = [pltpu.VMEM(array.shape, array.dtype) for array in stored]
     scratch += [
-        dma((len(stored), slots)),
+        dma((len(stored) + 1, slots)),
         pltpu.VMEM((2, slots) + cube, jnp.float32),
         pltpu.VMEM((2, slots, depth_cells * slab, lateral), jnp.bfloat16),
         pltpu.VMEM((2, slots, depth_cells * slab, lateral), jnp.bfloat16),
@@ -701,13 +726,13 @@
         spread[z, :, :wide] = np.eye(wide)
     spread = spread.reshape(cells, lanes) / float(wide * lateral)
     tables = [
-        spread,
         np.concatenate([cos_y, -sin_y], axis=1),
         np.concatenate([cos_y, -sin_y], axis=0),
         np.concatenate([cos_ahead, sin_ahead], axis=0),
         np.concatenate([cos_ahead.T, sin_ahead.T], axis=0),
     ]
-    stored += [jnp.asarray(table, jnp.float32) for table in tables]
+    stored.append(jnp.asarray(spread, jnp.float32))
+    stored += [jnp.asarray(two_parts(table)) for table in tables]
     return run_steps(
         blocks, shots, True, direct, stored, mass_spectrum, (kept, slab, lateral)
     )

time: 72.1 us -> 67.6 us (0.938)
  Pallas kernels: 69.7 us -> 65.2 us
    pallas_call x1, Pallas kernels: 49.2 us -> 44.7 us  [run_steps(): pl.pallas_call(functools.partial(step_kernel, blocks, shots, fused, len(s...]
where the time goes in v3:
time: 67.6 us; the launch traced here: 67.4 us
  Pallas kernels  65.2 us (96%)
  local copies, waits for them, and re-layouts  1.57 us (2%)
    pallas_call x1, Pallas kernels, run_steps(): pl.pallas_call(functools.partial(step_kernel, blocks, shots, fused, len(s...  44.7 us
    pallas_call x1, Pallas kernels, inject_all(): pl.pallas_call(functools.partial(inject_kernel, slab, own_size, edge_size...  20.5 us
    unnamed x1, local copies, waits for them, and re-layouts  1.57 us

profile of v3, /device:TPU:25, one launch (start us, length us, event | category | flops | bytes accessed | tf_op | source)
XLA Modules:
  0.0 67.4 jit_solution(17346887806633617199)
XLA Ops:
  0.7 20.5 %shard_map.154 = (f32[4,5,512,256]{3,2,1,0:T(8,128)}, f32[4,256,256]{2,1,0:T(8,128)}, f32[4,32,16,256]{3,2,1,0:T(8,128)}) custom-call(s32[3,4,2048]{2,1,0:T(4,128)} %bitcast.3, f32[5,4,2048]{2,1,0:T(4,128)} %bitcast.2, s32[4,3]{1,0:T(4,128)} %sources_ref.1, s32[1]{0:T(128)S(6)} %copy.18.live_ref, bf16[128,128]{1,0:T(8,128)(2,1)} %constant.16.clone.tri_ref), custom_call_target="tpu_custom_call" | custom-call | tf_op jit(solution)/shard_map/pallas_call | solution.py:200
  21.1 44.7 %shard_map.155 = f32[8,16,256]{2,1,0:T(8,128)} custom-call(s32[4,4]{1,0:T(4,128)} %refs_0_.1, f32[32,16,256]{2,1,0:T(8,128)} %refs_1_.1, bf16[2,256,1024]{2,1,0:T(8,128)(2,1)} %constant.17.clone.refs_2_, bf16[512,256]{1,0:T(8,128)(2,1)} %constant.18.clone.refs_3_, f32[4,5,512,256]{3,2,1,0:T(8,128)} %get-tuple-element.8.refs_4_, ...), custom_call_target="tpu_custom_call" | custom-call | tf_op jit(solution)/shard_map/pallas_call | solution.py:637
  65.9 1.6 %copy.19 = f32[8,16,256]{2,1,0:T(8,128)} copy(f32[8,16,256]{2,1,0:T(8,128)} %shard_map.155) | data formatting | bytes 262144

commit v4 on v3

--- a/solution.py
+++ b/solution.py
@@ -94,9 +94,10 @@
     across = (lax.broadcasted_iota(jnp.int32, flat, 0) + start).astype(jnp.float32) - place[1]
     side = lax.broadcasted_iota(jnp.int32, flat, 1).astype(jnp.float32) - place[2]
     fade_flat = live * jnp.exp(-(across * across + side * side) * scale)
+    gap = lax.broadcasted_iota(jnp.int32, (depth_cells, lateral), 0).astype(jnp.float32) - place[0]
+    fade_depth = jnp.exp(-(gap * gap) * scale)
     for z in range(depth_cells):
-        gap = jnp.full(flat, z, jnp.float32) - place[0]
-        fade_ref[0, z] = live - jnp.exp(-(gap * gap) * scale) * fade_flat
+        fade_ref[0, z] = live - fade_depth[z : z + 1] * fade_flat
 
     depth = receivers_ref[0, pl.ds(s, 1), :]
     local = receivers_ref[1, pl.ds(s, 1), :] - start

time: 67.6 us -> 67.6 us (level)
  no operation moved by 1% of the time
where the time goes in v4:
time: 67.6 us; the launch traced here: 67.4 us
  Pallas kernels  65.2 us (96%)
  local copies, waits for them, and re-layouts  1.57 us (2%)
    pallas_call x1, Pallas kernels, run_steps(): pl.pallas_call(functools.partial(step_kernel, blocks, shots, fused, len(s...  44.7 us
    pallas_call x1, Pallas kernels, inject_all(): pl.pallas_call(functools.partial(inject_kernel, slab, own_size, edge_size...  20.4 us
    unnamed x1, local copies, waits for them, and re-layouts  1.57 us

profile of v4, /device:TPU:25, one launch (start us, length us, event | category | flops | bytes accessed | tf_op | source)
XLA Modules:
  0.0 67.4 jit_solution(7550835631460715963)
XLA Ops:
  0.7 20.4 %shard_map.154 = (f32[4,5,512,256]{3,2,1,0:T(8,128)}, f32[4,256,256]{2,1,0:T(8,128)}, f32[4,32,16,256]{3,2,1,0:T(8,128)}) custom-call(s32[3,4,2048]{2,1,0:T(4,128)} %bitcast.3, f32[5,4,2048]{2,1,0:T(4,128)} %bitcast.2, s32[4,3]{1,0:T(4,128)} %sources_ref.1, s32[1]{0:T(128)S(6)} %copy.18.live_ref, bf16[128,128]{1,0:T(8,128)(2,1)} %constant.16.clone.tri_ref), custom_call_target="tpu_custom_call" | custom-call | tf_op jit(solution)/shard_map/pallas_call | solution.py:201
  21.1 44.7 %shard_map.155 = f32[8,16,256]{2,1,0:T(8,128)} custom-call(s32[4,4]{1,0:T(4,128)} %refs_0_.1, f32[32,16,256]{2,1,0:T(8,128)} %refs_1_.1, bf16[2,256,1024]{2,1,0:T(8,128)(2,1)} %constant.17.clone.refs_2_, bf16[512,256]{1,0:T(8,128)(2,1)} %constant.18.clone.refs_3_, f32[4,5,512,256]{3,2,1,0:T(8,128)} %get-tuple-element.8.refs_4_, ...), custom_call_target="tpu_custom_call" | custom-call | tf_op jit(solution)/shard_map/pallas_call | solution.py:638
  65.8 1.6 %copy.19 = f32[8,16,256]{2,1,0:T(8,128)} copy(f32[8,16,256]{2,1,0:T(8,128)} %shard_map.155) | data formatting | bytes 262144
